TPU v7x, 32 devices: a whole 2x2x4 slice. The times are simulated.
32 devices in a mesh: dp: 4 (over y, x), space: 8 (over z, core).
Axes of the slice: x: 2, y: 2, z: 4, core: 2. Of those that a mesh axis runs over, the one named last changes fastest.
Arguments:
- node_scalar: bfloat16 [4096, 1024], P(('dp', 'space')), may hold values from -6 to 6
- node_vector: bfloat16 [3, 4096, 256], P(None, ('dp', 'space')), may hold values from -6 to 6
- edge_scalar: bfloat16 [4096, 960], P(('dp', 'space')), may hold values from -6 to 6
- edge_vector: bfloat16 [3, 122880], P(None, ('dp', 'space')), may hold values from -6 to 6
- neighbours: int32 [4096, 30], P(('dp', 'space')), may hold values from 0 to 255, as said below
- send_rows: int32 [32, 8, 16], P(('dp', 'space')), may hold values from -1 to 127, as said below
- complex_id: int32 [4096], P('dp'), may hold values 0 or 1
- cotangent: bfloat16 [4096, 512], P(('dp', 'space')), may hold values from -6 to 6
- w_node: bfloat16 [1024, 2048], replicated, may hold values from -0.1875 to 0.1875
- w_edge: bfloat16 [32, 1024], replicated, may hold values from -1 to 1
- w_norms: bfloat16 [513, 1024], replicated, may hold values from -0.25 to 0.25
- vec_node: bfloat16 [256, 1026], replicated, may hold values from -0.375 to 0.375
- vec_edge: bfloat16 [1, 513], replicated, may hold values from -6 to 6
- vec_out: bfloat16 [513, 256], replicated, may hold values from -0.25 to 0.25
- norm_gain: bfloat16 [1024], replicated, may hold values from 0.5 to 1.5
- ff_vec: bfloat16 [256, 256], replicated, may hold values from -0.375 to 0.375
- ff_scalar: bfloat16 [1280, 1024], replicated, may hold values from -0.15625 to 0.15625
- ff_up: bfloat16 [256, 256], replicated, may hold values from -0.375 to 0.375
- w_embed: bfloat16 [1280, 512], replicated, may hold values from -0.15625 to 0.15625
- attn_gain: bfloat16 [512], replicated, may hold values from 0.5 to 1.5
- w_qkv: bfloat16 [512, 1536], replicated, may hold values from -0.25 to 0.25
- w_out: bfloat16 [512, 512], replicated, may hold values from -6 to 6
- ffn_gain: bfloat16 [512], replicated, may hold values from 0.5 to 1.5
- w_up: bfloat16 [512, 2048], replicated, may hold values from -0.25 to 0.25
- w_down: bfloat16 [2048, 512], replicated, may hold values from -0.125 to 0.125
Outputs:
- stream_out: bfloat16 [4096, 512], P(('dp', 'space'))
- grad_scalar: bfloat16 [4096, 1024], P(('dp', 'space'))
- grad_vector: bfloat16 [3, 4096, 256], P(None, ('dp', 'space'))
- grad_w_node: float32 [1024, 2048], P('space')
- grad_w_edge: float32 [32, 1024], P(None, 'space')
- grad_w_norms: float32 [513, 1024], P(None, 'space')
- grad_vec_node: float32 [256, 1026], P('space')
- grad_vec_edge: float32 [1, 513], replicated
- grad_vec_out: float32 [513, 256], P(None, 'space')
- grad_norm_gain: float32 [1024], P('space')
- grad_ff_vec: float32 [256, 256], P('space')
- grad_ff_scalar: float32 [1280, 1024], P('space')
- grad_ff_up: float32 [256, 256], P('space')
- grad_w_embed: float32 [1280, 512], P('space')
- grad_attn_gain: float32 [512], P('space')
- grad_w_qkv: float32 [512, 1536], P('space')
- grad_w_out: float32 [512, 512], P('space')
- grad_ffn_gain: float32 [512], P('space')
- grad_w_up: float32 [512, 2048], P('space')
- grad_w_down: float32 [2048, 512], P('space')
Inputs may be any that keep to these rules, and one draw needn't show every extreme that they name: `neighbours`: an entry below 128 is a row of the residue's own device; any other entry is 128 + d * 16 + c with send_rows[d, p, c] not -1 (a live slot sent to this device p by device d of the same batch). For device q of a space group, send_rows[q, d] holds the rows sent to device d: the live ones first, then -1. Rows may repeat. Blocks form a periodic cube grid of 8 blocks; live rows go only to the up to 26 adjacent blocks, between 8 and 16 to each, and some pair has 16 in every draw.
All inputs are finite; a program needn't handle non-finite values. No bound on the sum of `complex_id` on one device may be relied on, other than what follows from the above.
Results may differ from a plain program's by a relative error of at most 0.018.
Values may be sent and summed in bfloat16 or wider, within the bound.
A program may use at most 320 MiB of HBM per device.

v0:
```python
import math

import jax
import jax.numpy as jnp
from jax import lax
from jax.sharding import PartitionSpec as P

D_S = 1024
D_V = 256
H_V = 513
D_E = 32
NEIGH = 30
D_MODEL = 512
HEADS = 8
HEAD_DIM = 64
CAP = 16


def layer_norm(values, gain_row):
    centred = values - jnp.mean(values, axis=-1, keepdims=True)
    spread = jnp.mean(centred * centred, axis=-1, keepdims=True)
    return centred * lax.rsqrt(spread + 1e-05) * gain_row


def vector_norm(vectors):
    mean_power = jnp.mean(jnp.sum(vectors * vectors, axis=0), axis=-1, keepdims=True)
    return vectors * lax.rsqrt(mean_power + 1e-05)[None]


def length_plus(vectors):
    return jnp.sqrt(jnp.sum(vectors * vectors, axis=0) + 1.0)


def vector_gate(vectors):
    return vectors * jax.nn.sigmoid(length_plus(vectors))[None]


def gelu_exact(values):
    return jax.nn.gelu(values, approximate=False)


def product(former, latter):
    return jnp.dot(former, latter, preferred_element_type=jnp.float32)


def product_lead(former, latter):
    leading = tuple(range(former.ndim - 1))
    return lax.dot_general(
        former, latter, ((leading, leading), ((), ())), preferred_element_type=jnp.float32
    )


def product_back(former, latter):
    return lax.dot_general(
        former, latter, (((former.ndim - 1,), (1,)), ((), ())), preferred_element_type=jnp.float32
    )


def pullback(function, at_point, cotangent_in):
    unused, puller = jax.vjp(function, at_point)
    return puller(cotangent_in)[0]


def body(
    node_scalar,
    node_vector,
    edge_scalar,
    edge_vector,
    neighbours,
    send_rows,
    complex_id,
    cotangent,
    w_node,
    w_edge,
    w_norms,
    vec_node,
    vec_edge,
    vec_out,
    norm_gain,
    ff_vec,
    ff_scalar,
    ff_up,
    w_embed,
    attn_gain,
    w_qkv,
    w_out,
    ffn_gain,
    w_up,
    w_down,
):
    bfloat = jnp.bfloat16
    single = jnp.float32
    local_rows = node_scalar.shape[0]
    spaces = lax.axis_size("space")
    extra_rows = spaces * CAP
    all_nodes = complex_id.shape[0]
    sent_index = send_rows[0].reshape(-1)
    sent_live = sent_index >= 0
    sent_safe = jnp.maximum(sent_index, 0)
    vector_rows = jnp.moveaxis(node_vector, 0, 1)
    send_scalar = jnp.where(sent_live[:, None], node_scalar[sent_safe], 0)
    send_scalar = send_scalar.reshape(spaces, CAP, D_S)
    send_vector = jnp.where(sent_live[:, None, None], vector_rows[sent_safe], 0)
    send_vector = send_vector.reshape(spaces, CAP, 3 * D_V)
    recv_scalar, recv_vector = (
        lax.all_to_all(send_scalar, "space", split_axis=0, concat_axis=0, tiled=True),
        lax.all_to_all(send_vector, "space", split_axis=0, concat_axis=0, tiled=True),
    )
    table_s = jnp.concatenate([node_scalar, recv_scalar.reshape(extra_rows, D_S)], 0)
    table_v = jnp.concatenate(
        [node_vector, jnp.moveaxis(recv_vector.reshape(extra_rows, 3, D_V), 1, 0)], 1
    )
    a_source = product(table_s, w_node[:, :D_S])
    b_target = product(node_scalar, w_node[:, D_S:])
    p_source = product(table_v, vec_node[:, :H_V])
    q_target = product(node_vector, vec_node[:, H_V:])
    edge_gain = vec_edge[0].astype(single)
    block_rows = math.gcd(local_rows, 32)
    block_count = local_rows // block_rows
    block_starts = jnp.arange(block_count, dtype=jnp.int32) * block_rows

    def edge_forward(first_row):
        nearby = lax.dynamic_slice_in_dim(neighbours, first_row, block_rows, 0)
        scalars_in = lax.dynamic_slice_in_dim(edge_scalar, first_row, block_rows, 0).reshape(
            block_rows, NEIGH, D_E
        )
        vectors_in = lax.dynamic_slice_in_dim(edge_vector, first_row * NEIGH, block_rows * NEIGH, 1)
        vectors_in = vectors_in.reshape(3, block_rows, NEIGH).astype(single)
        target_b = lax.dynamic_slice_in_dim(b_target, first_row, block_rows, 0)
        target_q = lax.dynamic_slice_in_dim(q_target, first_row, block_rows, 1)
        hidden_v = p_source[:, nearby] + target_q[:, :, None] + vectors_in[..., None] * edge_gain
        lengths = length_plus(hidden_v)
        hidden_r = hidden_v.astype(bfloat)
        lengths_r = lengths.astype(bfloat)
        preact = (
            a_source[nearby]
            + target_b[:, None]
            + product(scalars_in, w_edge)
            + product(lengths_r, w_norms)
        )
        update = product(hidden_r, vec_out)
        return (nearby, scalars_in, vectors_in, hidden_v, hidden_r, lengths_r, preact, update)

    def edge_message(first_row):
        pieces = edge_forward(first_row)
        return (jnp.mean(jax.nn.silu(pieces[6]), axis=1), jnp.mean(vector_gate(pieces[7]), axis=2))

    agg_blocks, aggv_blocks = lax.map(edge_message, block_starts)
    agg_s = agg_blocks.reshape(local_rows, D_S)
    agg_v = jnp.moveaxis(aggv_blocks, 0, 1).reshape(3, local_rows, D_V)
    scalar_one = node_scalar.astype(single) + agg_s
    vector_one = node_vector.astype(single) + agg_v
    gain_norm = norm_gain.astype(single)
    normed_s = layer_norm(scalar_one, gain_norm)
    normed_v = vector_norm(vector_one)
    normed_vr = normed_v.astype(bfloat)
    ff_hidden = product(normed_vr, ff_vec)
    ff_hidden_r = ff_hidden.astype(bfloat)
    ff_length = length_plus(ff_hidden)
    ff_input = jnp.concatenate([normed_s.astype(bfloat), ff_length.astype(bfloat)], -1)
    ff_preact = product(ff_input, ff_scalar)
    ff_update = product(ff_hidden_r, ff_up)
    scalar_two = normed_s + jax.nn.silu(ff_preact)
    vector_two = normed_v + vector_gate(ff_update)
    embed_input = jnp.concatenate(
        [scalar_two.astype(bfloat), length_plus(vector_two).astype(bfloat)], -1
    )
    stream_zero = product(embed_input, w_embed)
    gain_attn = attn_gain.astype(single)
    attn_in = layer_norm(stream_zero, gain_attn).astype(bfloat)
    qkv_rounded = product(attn_in, w_qkv).astype(bfloat)
    queries = qkv_rounded[:, :D_MODEL]
    keys_local = qkv_rounded[:, D_MODEL : 2 * D_MODEL]
    values_local = qkv_rounded[:, 2 * D_MODEL :]
    full_keys, full_values = (
        lax.all_gather(keys_local, "space", axis=0, tiled=True),
        lax.all_gather(values_local, "space", axis=0, tiled=True),
    )
    position = lax.axis_index("space")
    query_ids = lax.dynamic_slice_in_dim(complex_id, position * local_rows, local_rows, 0)
    score_scale = HEAD_DIM ** (-0.5)
    query_heads = queries.reshape(local_rows, HEADS, HEAD_DIM)
    scores = (
        jnp.einsum(
            "qhd,khd->hqk",
            query_heads,
            full_keys.reshape(all_nodes, HEADS, HEAD_DIM),
            preferred_element_type=single,
        )
        * score_scale
    )
    scores = jnp.where((query_ids[:, None] == complex_id[None, :])[None], scores, -1000000000.0)
    row_peak = jnp.max(scores, axis=-1, keepdims=True)
    shifted = jnp.exp(scores - row_peak)
    totals = jnp.sum(shifted, axis=-1, keepdims=True)
    probs = shifted / totals
    log_total = row_peak + jnp.log(totals)
    attended = jnp.einsum(
        "hqk,khd->qhd",
        probs.astype(bfloat),
        full_values.reshape(all_nodes, HEADS, HEAD_DIM),
        preferred_element_type=single,
    ).reshape(local_rows, D_MODEL)
    attended_r = attended.astype(bfloat)
    stream_one = stream_zero + product(attended_r, w_out)
    gain_ffn = ffn_gain.astype(single)
    ffn_in = layer_norm(stream_one, gain_ffn).astype(bfloat)
    hidden_up = product(ffn_in, w_up)
    gelu_r = gelu_exact(hidden_up).astype(bfloat)
    stream_out = (stream_one + product(gelu_r, w_down)).astype(bfloat)
    grad_w_down = product_lead(gelu_r, cotangent)
    grad_gelu = product_back(cotangent, w_down)
    grad_up_r = pullback(gelu_exact, hidden_up, grad_gelu).astype(bfloat)
    grad_w_up = product_lead(ffn_in, grad_up_r)
    grad_ffn_in = product_back(grad_up_r, w_up)
    unused, ffn_pull = jax.vjp(layer_norm, stream_one, gain_ffn)
    grad_stream_ln, grad_ffn_gain = ffn_pull(grad_ffn_in)
    grad_stream_one = cotangent.astype(single) + grad_stream_ln
    grad_branch = grad_stream_one.astype(bfloat)
    grad_w_out = product_lead(attended_r, grad_branch)
    grad_attended = product_back(grad_branch, w_out).astype(bfloat)
    grad_heads = grad_attended.reshape(local_rows, HEADS, HEAD_DIM)
    row_dots = jnp.sum(
        grad_heads.astype(single) * attended.reshape(local_rows, HEADS, HEAD_DIM), axis=-1
    )
    row_dots = row_dots.T[:, :, None]
    key_block = local_rows * min(8, spaces)
    key_count = all_nodes // key_block

    def key_step(grad_query, block_index):
        first_key = block_index * key_block
        block_keys = lax.dynamic_slice_in_dim(full_keys, first_key, key_block, 0).reshape(
            key_block, HEADS, HEAD_DIM
        )
        block_values = lax.dynamic_slice_in_dim(full_values, first_key, key_block, 0)
        block_values = block_values.reshape(key_block, HEADS, HEAD_DIM)
        block_ids = lax.dynamic_slice_in_dim(complex_id, first_key, key_block, 0)
        block_scores = (
            jnp.einsum("qhd,khd->hqk", query_heads, block_keys, preferred_element_type=single)
            * score_scale
        )
        block_scores = jnp.where(
            (query_ids[:, None] == block_ids[None, :])[None], block_scores, -1000000000.0
        )
        block_probs = jnp.exp(block_scores - log_total)
        grad_probs = jnp.einsum(
            "qhd,khd->hqk", grad_heads, block_values, preferred_element_type=single
        )
        grad_scores = (block_probs * (grad_probs - row_dots)).astype(bfloat)
        grad_query = grad_query + jnp.einsum(
            "hqk,khd->qhd", grad_scores, block_keys, preferred_element_type=single
        )
        grad_keys = (
            jnp.einsum("hqk,qhd->khd", grad_scores, query_heads, preferred_element_type=single)
            * score_scale
        )
        grad_values = jnp.einsum(
            "hqk,qhd->khd", block_probs.astype(bfloat), grad_heads, preferred_element_type=single
        )
        return (
            grad_query,
            (grad_keys.reshape(key_block, D_MODEL), grad_values.reshape(key_block, D_MODEL)),
        )

    grad_query, (kgrad_blocks, vgrad_blocks) = lax.scan(
        key_step,
        jnp.zeros((local_rows, HEADS, HEAD_DIM), single),
        jnp.arange(key_count, dtype=jnp.int32),
    )
    grad_keys_own, grad_values_own = (
        lax.psum_scatter(
            kgrad_blocks.reshape(all_nodes, D_MODEL), "space", scatter_dimension=0, tiled=True
        ),
        lax.psum_scatter(
            vgrad_blocks.reshape(all_nodes, D_MODEL), "space", scatter_dimension=0, tiled=True
        ),
    )
    grad_qkv = jnp.concatenate(
        [grad_query.reshape(local_rows, D_MODEL) * score_scale, grad_keys_own, grad_values_own], -1
    ).astype(bfloat)
    grad_w_qkv = product_lead(attn_in, grad_qkv)
    grad_attn_in = product_back(grad_qkv, w_qkv)
    unused, attn_pull = jax.vjp(layer_norm, stream_zero, gain_attn)
    grad_zero_ln, grad_attn_gain = attn_pull(grad_attn_in)
    grad_stream_r = (grad_stream_one + grad_zero_ln).astype(bfloat)
    grad_w_embed = product_lead(embed_input, grad_stream_r)
    grad_embed_in = product_back(grad_stream_r, w_embed)
    grad_vector_two = pullback(length_plus, vector_two, grad_embed_in[:, D_S:])
    grad_ff_pre = pullback(jax.nn.silu, ff_preact, grad_embed_in[:, :D_S]).astype(bfloat)
    grad_ff_scalar = product_lead(ff_input, grad_ff_pre)
    grad_ff_input = product_back(grad_ff_pre, ff_scalar)
    grad_ff_update = pullback(vector_gate, ff_update, grad_vector_two).astype(bfloat)
    grad_ff_up = product_lead(ff_hidden_r, grad_ff_update)
    grad_ff_hidden = (
        product_back(grad_ff_update, ff_up)
        + pullback(length_plus, ff_hidden, grad_ff_input[:, D_S:])
    ).astype(bfloat)
    grad_ff_vec = product_lead(normed_vr, grad_ff_hidden)
    grad_normed_v = grad_vector_two + product_back(grad_ff_hidden, ff_vec)
    grad_normed_s = grad_embed_in[:, :D_S] + grad_ff_input[:, :D_S]
    unused, norm_pull = jax.vjp(layer_norm, scalar_one, gain_norm)
    grad_scalar_one, grad_norm_gain = norm_pull(grad_normed_s)
    grad_vector_one = pullback(vector_norm, vector_one, grad_normed_v)

    def edge_back(running, first_row):
        grad_a, grad_p, grad_edge_w, grad_norm_w, grad_vout_w, grad_vedge = running
        nearby, scalars_in, vectors_in, hidden_v, hidden_r, lengths_r, preact, update = (
            edge_forward(first_row)
        )
        share_s = (
            lax.dynamic_slice_in_dim(grad_scalar_one, first_row, block_rows, 0)[:, None, :] / NEIGH
        )
        share_v = (
            lax.dynamic_slice_in_dim(grad_vector_one, first_row, block_rows, 1)[:, :, None, :]
            / NEIGH
        )
        grad_pre = pullback(jax.nn.silu, preact, jnp.broadcast_to(share_s, preact.shape)).astype(
            bfloat
        )
        grad_update = pullback(vector_gate, update, jnp.broadcast_to(share_v, update.shape)).astype(
            bfloat
        )
        grad_vout_w = grad_vout_w + product_lead(hidden_r, grad_update)
        grad_norm_w = grad_norm_w + product_lead(lengths_r, grad_pre)
        grad_edge_w = grad_edge_w + product_lead(scalars_in, grad_pre)
        grad_lengths = product_back(grad_pre, w_norms)
        grad_hidden = product_back(grad_update, vec_out) + pullback(
            length_plus, hidden_v, grad_lengths
        )
        grad_vedge = grad_vedge + jnp.einsum("cik,cikh->h", vectors_in, grad_hidden)
        grad_pre_single = grad_pre.astype(single)
        flat_nearby = nearby.reshape(-1)
        grad_a = grad_a.at[flat_nearby].add(grad_pre_single.reshape(-1, D_S))
        grad_p = grad_p.at[:, flat_nearby].add(grad_hidden.reshape(3, -1, H_V))
        running = (grad_a, grad_p, grad_edge_w, grad_norm_w, grad_vout_w, grad_vedge)
        return (running, (jnp.sum(grad_pre_single, axis=1), jnp.sum(grad_hidden, axis=2)))

    table_count = local_rows + extra_rows
    start_state = (
        jnp.zeros((table_count, D_S), single),
        jnp.zeros((3, table_count, H_V), single),
        jnp.zeros((D_E, D_S), single),
        jnp.zeros((H_V, D_S), single),
        jnp.zeros((H_V, D_V), single),
        jnp.zeros((H_V,), single),
    )
    final_state, (grad_b_blocks, grad_q_blocks) = lax.scan(edge_back, start_state, block_starts)
    grad_a, grad_p, grad_w_edge, grad_w_norms, grad_vec_out, grad_vedge = final_state
    grad_vec_edge = lax.psum(grad_vedge[None, :], ("dp", "space"))
    grad_a_r = grad_a.astype(bfloat)
    grad_p_r = grad_p.astype(bfloat)
    grad_b_r = grad_b_blocks.reshape(local_rows, D_S).astype(bfloat)
    grad_q_r = jnp.moveaxis(grad_q_blocks, 0, 1).reshape(3, local_rows, H_V).astype(bfloat)
    grad_w_node = jnp.concatenate(
        [product_lead(table_s, grad_a_r), product_lead(node_scalar, grad_b_r)], 1
    )
    grad_vec_node = jnp.concatenate(
        [product_lead(table_v, grad_p_r), product_lead(node_vector, grad_q_r)], 1
    )
    grad_table_scalar = product_back(grad_a_r, w_node[:, :D_S])
    grad_table_vector = product_back(grad_p_r, vec_node[:, :H_V])
    grad_scalar = (
        grad_scalar_one + product_back(grad_b_r, w_node[:, D_S:]) + grad_table_scalar[:local_rows]
    )
    grad_vector = (
        grad_vector_one
        + product_back(grad_q_r, vec_node[:, H_V:])
        + grad_table_vector[:, :local_rows]
    )
    back_scalar = grad_table_scalar[local_rows:].reshape(spaces, CAP, D_S)
    back_vector = jnp.moveaxis(grad_table_vector[:, local_rows:], 0, 1).reshape(
        spaces, CAP, 3 * D_V
    )
    got_scalar, got_vector = (
        lax.all_to_all(
            back_scalar.astype(jnp.bfloat16), "space", split_axis=0, concat_axis=0, tiled=True
        ).astype(back_scalar.dtype),
        lax.all_to_all(
            back_vector.astype(jnp.bfloat16), "space", split_axis=0, concat_axis=0, tiled=True
        ).astype(back_vector.dtype),
    )
    got_scalar = jnp.where(sent_live[:, None], got_scalar.reshape(extra_rows, D_S), 0.0)
    got_vector = jnp.where(sent_live[:, None, None], got_vector.reshape(extra_rows, 3, D_V), 0.0)
    grad_scalar = grad_scalar.at[sent_safe].add(got_scalar)
    vector_added = jnp.zeros((local_rows, 3, D_V), single).at[sent_safe].add(got_vector)
    grad_vector = grad_vector + jnp.moveaxis(vector_added, 1, 0)
    (
        grad_w_node,
        grad_w_edge,
        grad_w_norms,
        grad_vec_node,
        grad_vec_out,
        grad_norm_gain,
        grad_ff_vec,
        grad_ff_scalar,
        grad_ff_up,
        grad_w_embed,
        grad_attn_gain,
        grad_w_qkv,
        grad_w_out,
        grad_ffn_gain,
        grad_w_up,
        grad_w_down,
    ) = (
        lax.psum_scatter(grad_w_node, "space", scatter_dimension=0, tiled=True),
        lax.psum_scatter(grad_w_edge, "space", scatter_dimension=1, tiled=True),
        lax.psum_scatter(grad_w_norms, "space", scatter_dimension=1, tiled=True),
        lax.psum_scatter(grad_vec_node, "space", scatter_dimension=0, tiled=True),
        lax.psum_scatter(grad_vec_out, "space", scatter_dimension=1, tiled=True),
        lax.psum_scatter(grad_norm_gain, "space", scatter_dimension=0, tiled=True),
        lax.psum_scatter(grad_ff_vec, "space", scatter_dimension=0, tiled=True),
        lax.psum_scatter(grad_ff_scalar, "space", scatter_dimension=0, tiled=True),
        lax.psum_scatter(grad_ff_up, "space", scatter_dimension=0, tiled=True),
        lax.psum_scatter(grad_w_embed, "space", scatter_dimension=0, tiled=True),
        lax.psum_scatter(grad_attn_gain, "space", scatter_dimension=0, tiled=True),
        lax.psum_scatter(grad_w_qkv, "space", scatter_dimension=0, tiled=True),
        lax.psum_scatter(grad_w_out, "space", scatter_dimension=0, tiled=True),
        lax.psum_scatter(grad_ffn_gain, "space", scatter_dimension=0, tiled=True),
        lax.psum_scatter(grad_w_up, "space", scatter_dimension=0, tiled=True),
        lax.psum_scatter(grad_w_down, "space", scatter_dimension=0, tiled=True),
    )
    (
        grad_w_node,
        grad_w_edge,
        grad_w_norms,
        grad_vec_node,
        grad_vec_out,
        grad_norm_gain,
        grad_ff_vec,
        grad_ff_scalar,
        grad_ff_up,
        grad_w_embed,
        grad_attn_gain,
        grad_w_qkv,
        grad_w_out,
        grad_ffn_gain,
        grad_w_up,
        grad_w_down,
    ) = (
        lax.psum(grad_w_node.astype(jnp.bfloat16), "dp").astype(jnp.float32),
        lax.psum(grad_w_edge.astype(jnp.bfloat16), "dp").astype(jnp.float32),
        lax.psum(grad_w_norms.astype(jnp.bfloat16), "dp").astype(jnp.float32),
        lax.psum(grad_vec_node.astype(jnp.bfloat16), "dp").astype(jnp.float32),
        lax.psum(grad_vec_out.astype(jnp.bfloat16), "dp").astype(jnp.float32),
        lax.psum(grad_norm_gain.astype(jnp.bfloat16), "dp").astype(jnp.float32),
        lax.psum(grad_ff_vec.astype(jnp.bfloat16), "dp").astype(jnp.float32),
        lax.psum(grad_ff_scalar.astype(jnp.bfloat16), "dp").astype(jnp.float32),
        lax.psum(grad_ff_up.astype(jnp.bfloat16), "dp").astype(jnp.float32),
        lax.psum(grad_w_embed.astype(jnp.bfloat16), "dp").astype(jnp.float32),
        lax.psum(grad_attn_gain.astype(jnp.bfloat16), "dp").astype(jnp.float32),
        lax.psum(grad_w_qkv.astype(jnp.bfloat16), "dp").astype(jnp.float32),
        lax.psum(grad_w_out.astype(jnp.bfloat16), "dp").astype(jnp.float32),
        lax.psum(grad_ffn_gain.astype(jnp.bfloat16), "dp").astype(jnp.float32),
        lax.psum(grad_w_up.astype(jnp.bfloat16), "dp").astype(jnp.float32),
        lax.psum(grad_w_down.astype(jnp.bfloat16), "dp").astype(jnp.float32),
    )
    return (
        stream_out,
        grad_scalar.astype(bfloat),
        grad_vector.astype(bfloat),
        grad_w_node,
        grad_w_edge,
        grad_w_norms,
        grad_vec_node,
        grad_vec_edge,
        grad_vec_out,
        grad_norm_gain,
        grad_ff_vec,
        grad_ff_scalar,
        grad_ff_up,
        grad_w_embed,
        grad_attn_gain,
        grad_w_qkv,
        grad_w_out,
        grad_ffn_gain,
        grad_w_up,
        grad_w_down,
    )


def solution(mesh):
    return jax.shard_map(
        body,
        mesh=mesh,
        in_specs=(
            P(("dp", "space"), None),
            P(None, ("dp", "space"), None),
            P(("dp", "space"), None),
            P(None, ("dp", "space")),
            P(("dp", "space"), None),
            P(("dp", "space"), None, None),
            P("dp"),
            P(("dp", "space"), None),
            P(),
            P(),
            P(),
            P(),
            P(),
            P(),
            P(),
            P(),
            P(),
            P(),
            P(),
            P(),
            P(),
            P(),
            P(),
            P(),
            P(),
        ),
        out_specs=(
            P(("dp", "space"), None),
            P(("dp", "space"), None),
            P(None, ("dp", "space"), None),
            P("space", None),
            P(None, "space"),
            P(None, "space"),
            P("space", None),
            P(),
            P(None, "space"),
            P("space"),
            P("space", None),
            P("space", None),
            P("space", None),
            P("space", None),
            P("space"),
            P("space", None),
            P("space", None),
            P("space"),
            P("space", None),
            P("space", None),
        ),
        check_vma=False,
    )
```

profile of v0, /device:TPU:0, one launch (start us, length us, event | category | flops | bytes accessed | tf_op | source)
XLA Modules:
  0.0 2137.7 jit_solution(7306864424967409471)
XLA Ops:
  48.5 215.3 %while.45 = (s32[]{:T(128)}, f32[4,32,1024]{2,1,0:T(8,128)}, f32[4,3,32,256]{3,2,1,0:T(8,128)}, s32[4]{0:T(128)S(1)}, s32[128,30]{1,0:T(8,128)}, /*index=5*/f32[...) while((s32[]{:T(128)}, f32[4,32,1024]{2,1,0:T(8,128)}, ...), condition=%wide.region_5.6_spmd.clone, body=%wide.region_0.5_spmd.sunk.clone | while | flops 1848877568 | bytes 89341344 | solution.py:148
  70.2 16.9 gather_fusion
  123.9 16.9 gather_fusion
  177.7 16.9 gather_fusion
  231.4 16.9 gather_fusion
  278.4 19.7 all-gather.5.cloned.1.call-done
  306.9 15.1 all-gather.3.cloned.1.call-done
  358.2 22.4 %reduce-scatter.20.cloned.1.call-done = f32[128,512]{0,1:T(8,128)} async-done(((f32[1024,512]{0,1:T(8,128)}), f32[128,512]{0,1:T(8,128)}) %reduce-scatter.20.cloned.1.call-update) | async-done | bytes 262160 | tf_op jit(solution)/shard_map/reduce_scatter | solution.py:274
  382.2 35.1 %reduce-scatter.18.cloned.1.call-done = f32[128,512]{0,1:T(8,128)} async-done(((f32[1024,512]{0,1:T(8,128)}), f32[128,512]{0,1:T(8,128)}) %reduce-scatter.18.cloned.1.call-update) | async-done | bytes 262160 | tf_op jit(solution)/shard_map/reduce_scatter | solution.py:271
  433.0 996.1 %while.46 = (s32[]{:T(128)}, f32[256,1024]{1,0:T(8,128)S(1)}, f32[3,256,513]{2,0,1:T(4,128)}, f32[32,1024]{1,0:T(8,128)}, f32[513,1024]{1,0:T(8,128)}, /*index=5...) while((s32[]{:T(128)}, f32[256,1024]{1,0:T(8,128)S(1)}, ...), condition=%wide.region_37.38_spmd.clone.clone, body=%wide.region_29.37_spmd.clone.sunk.clone | while | flops 5483356672 | bytes 279535680 | solution.py:347
  453.4 16.9 gather_fusion.2
  552.4 126.7 %scatter_fusion.1 = f32[3,256,513]{2,0,1:T(4,128)} fusion(f32[3,256,513]{2,0,1:T(4,128)} %get-tuple-element.1162, s32[960]{0:T(1024)S(1)} %bitcast.359, f32[960,3,513]{2,1,0:T(4,128)} %copy.309), kind=kCustom, calls=%fused_computation.7.clone.clone.1.clone | custom fusion | flops 1477440 | bytes 17733120 | tf_op jit(solution)/shard_map/while/body/eval_jaxpr/scatter-add | solution.py:334
  699.4 16.9 gather_fusion.2
  799.6 126.7 %scatter_fusion.1 = f32[3,256,513]{2,0,1:T(4,128)} fusion(f32[3,256,513]{2,0,1:T(4,128)} %get-tuple-element.1162, s32[960]{0:T(1024)S(1)} %bitcast.359, f32[960,3,513]{2,1,0:T(4,128)} %copy.309), kind=kCustom, calls=%fused_computation.7.clone.clone.1.clone | custom fusion | flops 1477440 | bytes 17733120 | tf_op jit(solution)/shard_map/while/body/eval_jaxpr/scatter-add | solution.py:334
  946.9 16.9 gather_fusion.2
  1047.1 126.7 %scatter_fusion.1 = f32[3,256,513]{2,0,1:T(4,128)} fusion(f32[3,256,513]{2,0,1:T(4,128)} %get-tuple-element.1162, s32[960]{0:T(1024)S(1)} %bitcast.359, f32[960,3,513]{2,1,0:T(4,128)} %copy.309), kind=kCustom, calls=%fused_computation.7.clone.clone.1.clone | custom fusion | flops 1477440 | bytes 17733120 | tf_op jit(solution)/shard_map/while/body/eval_jaxpr/scatter-add | solution.py:334
  1194.0 16.9 gather_fusion.2
  1294.2 126.7 %scatter_fusion.1 = f32[3,256,513]{2,0,1:T(4,128)} fusion(f32[3,256,513]{2,0,1:T(4,128)} %get-tuple-element.1162, s32[960]{0:T(1024)S(1)} %bitcast.359, f32[960,3,513]{2,1,0:T(4,128)} %copy.309), kind=kCustom, calls=%fused_computation.7.clone.clone.1.clone | custom fusion | flops 1477440 | bytes 17733120 | tf_op jit(solution)/shard_map/while/body/eval_jaxpr/scatter-add | solution.py:334
  1475.5 15.0 all-reduce.3
  1494.9 26.0 %reduce-scatter.30.cloned.1.call-done = f32[32,256]{1,0:T(8,128)} async-done(((f32[256,256]{1,0:T(8,128)}), f32[32,256]{1,0:T(8,128)}) %reduce-scatter.30.cloned.1.call-update) | async-done | bytes 32784 | tf_op jit(solution)/shard_map/reduce_scatter | solution.py:411
  1522.3 31.1 %reduce-scatter.28.cloned.1.call-done = f32[513,32]{0,1:T(8,128)} async-done(((f32[513,256]{0,1:T(8,128)}), f32[513,32]{0,1:T(8,128)}) %reduce-scatter.28.cloned.1.call-update) | async-done | bytes 65680 | tf_op jit(solution)/shard_map/reduce_scatter | solution.py:409
  1555.0 31.9 %reduce-scatter.40.cloned.1.call-done = f32[64,512]{1,0:T(8,128)} async-done(((f32[512,512]{1,0:T(8,128)}), f32[64,512]{1,0:T(8,128)}) %reduce-scatter.40.cloned.1.call-update) | async-done | bytes 131088 | tf_op jit(solution)/shard_map/reduce_scatter | solution.py:417
  1588.4 31.7 %reduce-scatter.46.cloned.1.call-done = f32[32,1026]{1,0:T(8,128)} async-done(((f32[256,1026]{1,0:T(8,128)}), f32[32,1026]{1,0:T(8,128)}) %reduce-scatter.46.cloned.1.call-update) | async-done | bytes 131344
  1621.9 48.9 %reduce-scatter.42.cloned.1.call-done = f32[64,2048]{1,0:T(8,128)} async-done(((f32[512,2048]{1,0:T(8,128)}), f32[64,2048]{1,0:T(8,128)}) %reduce-scatter.42.cloned.1.call-update) | async-done | bytes 524304 | tf_op jit(solution)/shard_map/reduce_scatter | solution.py:419
  1672.5 48.7 %reduce-scatter.44.cloned.1.call-done = f32[256,512]{1,0:T(8,128)} async-done(((f32[2048,512]{1,0:T(8,128)}), f32[256,512]{1,0:T(8,128)}) %reduce-scatter.44.cloned.1.call-update) | async-done | bytes 524304 | tf_op jit(solution)/shard_map/reduce_scatter | solution.py:420
  1723.0 34.7 %reduce-scatter.26.cloned.1.call-done = f32[513,128]{1,0:T(8,128)} async-done(((f32[513,1024]{1,0:T(8,128)}), f32[513,128]{1,0:T(8,128)}) %reduce-scatter.26.cloned.1.call-update) | async-done | bytes 262672 | tf_op jit(solution)/shard_map/reduce_scatter | solution.py:407
  1759.3 37.1 %reduce-scatter.36.cloned.1.call-done = f32[160,512]{1,0:T(8,128)} async-done(((f32[1280,512]{1,0:T(8,128)}), f32[160,512]{1,0:T(8,128)}) %reduce-scatter.36.cloned.1.call-update) | async-done | bytes 327696 | tf_op jit(solution)/shard_map/reduce_scatter | solution.py:414
  1798.0 40.0 %reduce-scatter.38.cloned.1.call-done = f32[64,1536]{1,0:T(8,128)} async-done(((f32[512,1536]{1,0:T(8,128)}), f32[64,1536]{1,0:T(8,128)}) %reduce-scatter.38.cloned.1.call-update) | async-done | bytes 393232 | tf_op jit(solution)/shard_map/reduce_scatter | solution.py:416
  1839.7 59.6 %reduce-scatter.32.cloned.1.call-done = f32[160,1024]{1,0:T(8,128)} async-done(((f32[1280,1024]{1,0:T(8,128)}), f32[160,1024]{1,0:T(8,128)}) %reduce-scatter.32.cloned.1.call-update) | async-done | bytes 655376 | tf_op jit(solution)/shard_map/reduce_scatter | solution.py:412
  1901.1 88.4 %reduce-scatter.22.cloned.1.call-done = f32[128,2048]{0,1:T(8,128)} async-done(((f32[1024,2048]{0,1:T(8,128)}), f32[128,2048]{0,1:T(8,128)}) %reduce-scatter.22.cloned.1.call-update) | async-done | bytes 1048592 | tf_op jit(solution)/shard_map/reduce_scatter | solution.py:405
  2005.6 40.7 %psum.123 = f32[1,513]{1,0:T(1,128)} all-reduce(f32[1,513]{1,0:T(1,128)S(1)} %broadcast_in_dim.254), channel_id=1, replica_groups=mesh['dp'=4,'space'=8] {'dp','space'}, use_global_device_ids=true, to_apply=%region_48.49 | all-reduce | flops 513 | bytes 4104 | tf_op jit(solution)/shard_map/psum | solution.py:349
  2077.5 39.3 %all-reduce.11.cloned.1.call-done = (bf16[128,2048]{0,1:T(8,128)(2,1)}, bf16[32,1026]{0,1:T(8,128)(2,1)}, bf16[513,128]{1,0:T(8,128)(2,1)}, bf16[160,1024]{1,0:T...) async-done(((bf16[128,2048]{0,1:T(8,128)(2,1)}, ...) | async-done | bytes 1999248 | tf_op jit(solution)/shard_map/psum | solution.py:440
  (856 shorter events, 781.0 us)
Async XLA Ops:
  7.2 263.2 %copy-start = (bf16[1280,1024]{1,0:T(8,128)(2,1)S(1)}, bf16[1280,1024]{1,0:T(8,128)(2,1)}, u32[]{:S(2)}) copy-start(bf16[1280,1024]{1,0:T(8,128)(2,1)} %param.45) | copy-start | bytes 7864324
  11.8 17.8 all-to-all-start.1
  29.6 15.5 all-to-all-start
  34.7 263.3 %all-gather.5.cloned.1.call-start = ((), (), s32[]{:S(2)}) async-start(), calls=%async_computation.20 | async-start | bytes 1179648 | tf_op jit(solution)/shard_map/all_gather | solution.py:176
  48.5 216.5 %copy-start.22 = (bf16[3,128,256]{2,1,0:T(8,128)(2,1)S(1)}, bf16[3,128,256]{2,1,0:T(8,128)(2,1)}, u32[]{:S(2)}) copy-start(bf16[3,128,256]{2,1,0:T(8,128)(2,1)} %param.30) | copy-start | bytes 589828
  265.1 164.1 %copy-start.10 = (f32[3,128,256]{2,1,0:T(8,128)}, f32[3,128,256]{2,1,0:T(8,128)S(1)}, u32[]{:S(2)}) copy-start(f32[3,128,256]{2,1,0:T(8,128)S(1)} %get-tuple-element.688) | copy-start | bytes 1179652
  274.3 47.6 %all-gather.3.cloned.1.call-start = ((), (), s32[]{:S(2)}) async-start(), calls=%async_computation.19 | async-start | bytes 1179648 | tf_op jit(solution)/shard_map/all_gather | solution.py:177
  275.1 105.5 %reduce-scatter.20.cloned.1.call-start = ((), (), s32[]{:S(2)}) async-start(), calls=%async_computation.22 | async-start | bytes 2359296 | tf_op jit(solution)/shard_map/reduce_scatter | solution.py:274
  275.8 60.0 %copy-start.95 = (f32[512]{0:T(512)}, f32[512]{0:T(512)S(1)}, u32[]{:S(2)}) copy-start(f32[512]{0:T(512)S(1)} %convert_element_type.294) | copy-start | bytes 6148
  345.0 72.3 %reduce-scatter.18.cloned.1.call-start = ((), (), s32[]{:S(2)}) async-start(), calls=%async_computation.21 | async-start | bytes 2359296 | tf_op jit(solution)/shard_map/reduce_scatter | solution.py:271
  353.9 64.5 %copy-start.99 = (f32[512]{0:T(512)S(1)}, f32[512]{0:T(512)}, u32[]{:S(2)}) copy-start(f32[512]{0:T(512)} %convert_element_type.288) | copy-start | bytes 6148
  353.9 1138.3 %reduce-scatter.24.cloned.1.call-start = ((), (), s32[]{:S(2)}) async-start(), calls=%async_computation.24 | async-start | bytes 147456 | tf_op jit(solution)/shard_map/reduce_scatter | solution.py:406
  433.0 998.4 %copy-start.11 = (f32[3,128,256]{2,1,0:T(8,128)S(1)}, f32[3,128,256]{2,1,0:T(8,128)}, u32[]{:S(2)}) copy-start(f32[3,128,256]{2,1,0:T(8,128)} %copy-done.10) | copy-start | bytes 1179652
  433.0 998.4 %copy-start.103 = (f32[128]{0:T(128)S(1)}, f32[128]{0:T(128)}, u32[]{:S(2)}) copy-start(f32[128]{0:T(128)} %copy-done.101) | copy-start | bytes 1540
  1429.2 64.4 %reduce-scatter.34.cloned.1.call-start = ((), (), s32[]{:S(2)}) async-start(), calls=%async_computation.29 | async-start | bytes 294912 | tf_op jit(solution)/shard_map/reduce_scatter | solution.py:413
  1431.4 89.6 %reduce-scatter.30.cloned.1.call-start = ((), (), s32[]{:S(2)}) async-start(), calls=%async_computation.27 | async-start | bytes 294912 | tf_op jit(solution)/shard_map/reduce_scatter | solution.py:411
  1433.4 120.0 %reduce-scatter.28.cloned.1.call-start = ((), (), s32[]{:S(2)}) async-start(), calls=%async_computation.26 | async-start | bytes 737280 | tf_op jit(solution)/shard_map/reduce_scatter | solution.py:409
  1435.6 151.3 %reduce-scatter.40.cloned.1.call-start = ((), (), s32[]{:S(2)}) async-start(), calls=%async_computation.32 | async-start | bytes 1179648 | tf_op jit(solution)/shard_map/reduce_scatter | solution.py:417
  1437.0 183.1 %reduce-scatter.46.cloned.1.call-start = ((), (), s32[]{:S(2)}) async-start(), calls=%async_computation.35 | async-start | bytes 1327104
  1447.1 223.6 %reduce-scatter.42.cloned.1.call-start = ((), (), s32[]{:S(2)}) async-start(), calls=%async_computation.33 | async-start | bytes 4718592 | tf_op jit(solution)/shard_map/reduce_scatter | solution.py:419
  1451.1 270.1 %reduce-scatter.44.cloned.1.call-start = ((), (), s32[]{:S(2)}) async-start(), calls=%async_computation.34 | async-start | bytes 4718592 | tf_op jit(solution)/shard_map/reduce_scatter | solution.py:420
  1455.7 302.0 %reduce-scatter.26.cloned.1.call-start = ((), (), s32[]{:S(2)}) async-start(), calls=%async_computation.25 | async-start | bytes 2396160 | tf_op jit(solution)/shard_map/reduce_scatter | solution.py:407
  1456.4 339.9 %reduce-scatter.36.cloned.1.call-start = ((), (), s32[]{:S(2)}) async-start(), calls=%async_computation.30 | async-start | bytes 2949120 | tf_op jit(solution)/shard_map/reduce_scatter | solution.py:414
  1458.6 379.4 %reduce-scatter.38.cloned.1.call-start = ((), (), s32[]{:S(2)}) async-start(), calls=%async_computation.31 | async-start | bytes 3538944 | tf_op jit(solution)/shard_map/reduce_scatter | solution.py:416
  1461.2 438.1 %reduce-scatter.32.cloned.1.call-start = ((), (), s32[]{:S(2)}) async-start(), calls=%async_computation.28 | async-start | bytes 5898240 | tf_op jit(solution)/shard_map/reduce_scatter | solution.py:412
  1465.4 524.2 %reduce-scatter.22.cloned.1.call-start = ((), (), s32[]{:S(2)}) async-start(), calls=%async_computation.23 | async-start | bytes 9437184 | tf_op jit(solution)/shard_map/reduce_scatter | solution.py:405
  1473.0 595.5 %all-reduce.9.cloned.1.call-start = ((), (), s32[]{:S(2)}) async-start(), calls=%async_computation.36 | async-start | bytes 166912 | tf_op jit(solution)/shard_map/psum | solution.py:441
  1554.9 561.8 %all-reduce.11.cloned.1.call-start = ((), (), s32[]{:S(2)}) async-start(), calls=%async_computation.37 | async-start | bytes 4399104 | tf_op jit(solution)/shard_map/psum | solution.py:440
  1621.9 369.7 %copy-start.97 = (s32[1,8,16]{2,1,0:T(8,128)S(1)}, s32[1,8,16]{2,1,0:T(8,128)}, u32[]{:S(2)}) copy-start(s32[1,8,16]{2,1,0:T(8,128)} %param.34) | copy-start | bytes 1540
  1998.2 51.4 %all-to-all-start.3 = ((bf16[8,16,768]{2,1,0:T(8,128)(2,1)}), bf16[8,16,768]{2,1,0:T(8,128)(2,1)}, u32[]{:S(2)}, u32[]{:S(2)}) async-start(bf16[8,16,768]{2,1,0:T(8,128)(2,1)} %convert_element_type.319), calls=%async_computation.5 | async-start | bytes 393216 | tf_op jit(solution)/shard_map/all_to_all | solution.py:378
  2049.6 13.6 all-to-all-start.2
  2063.1 67.7 %copy-start.1 = (bf16[1280,1024]{1,0:T(8,128)(2,1)S(1)}, bf16[1280,1024]{1,0:T(8,128)(2,1)}, u32[]{:S(2)}) copy-start(bf16[1280,1024]{1,0:T(8,128)(2,1)} %param.45) | copy-start | bytes 7864324
  (186 other events, 829.1 us)
Sparse Core Ops, SparseCore 0:
  274.5 23.5 all-gather.4
  300.2 21.7 all-gather.2
  345.1 35.3 reduce-scatter.19
  382.7 34.5 reduce-scatter.17
  1429.3 28.9 reduce-scatter.23
  1461.0 28.5 reduce-scatter.33
  1492.4 28.4 reduce-scatter.29
  1523.9 29.4 reduce-scatter.27
  1556.4 30.4 reduce-scatter.39
  1589.1 30.9 reduce-scatter.45
  1622.5 48.2 reduce-scatter.41
  1673.0 48.1 reduce-scatter.43
  1723.6 33.9 reduce-scatter.25
  1759.9 36.4 reduce-scatter.35
  1798.6 39.3 reduce-scatter.37
  1840.3 58.9 reduce-scatter.31
  1901.5 87.9 reduce-scatter.21
  1995.2 41.2 all-reduce.8
  2042.4 74.2 all-reduce.10
where the time goes:
time: 2150 us; the launch traced here: 2140 us
  other arithmetic  707 us (33%)
  waiting for transfers between devices  612 us (28%)
  local copies, waits for them, and re-layouts  464 us (22%)
  matrix products  229 us (11%)
  blocking collectives  55.6 us (3%)
  loops' own time  32 us (1%)
    scatter-add x4, other arithmetic, edge_back(): grad_p = grad_p.at[:, flat_nearby].add(grad_hidden.reshape(3, -1, H_V))  507 us
    gather x8, local copies, waits for them, and re-layouts, edge_forward(): p_source[:, nearby] + target_q[:, :, None]  136 us
    dot_general x36, matrix products, product(): return jnp.dot(former, latter, preferred_element_type=jnp.float32)  103 us
    gather x16, local copies, waits for them, and re-layouts, edge_forward(): a_source[nearby] + target_b[:, None] + product(scalars_in, w_edge)  88.6 us
    reduce_scatter x1, waiting for transfers between devices, body(): lax.psum_scatter(grad_w_node, 'space', scatter_dimension=0, tiled=True)  88.4 us
    reshape x8, local copies, waits for them, and re-layouts, edge_back(): grad_p = grad_p.at[:, flat_nearby].add(grad_hidden.reshape(3, -1, H_V))  79.5 us
    reduce_scatter x1, waiting for transfers between devices, body(): lax.psum_scatter(grad_ff_scalar, 'space', scatter_dimension=0, tiled=True)  59.6 us
    dot_general x24, matrix products, product_lead(): lax.dot_general(former, latter, ((leading, leading), ((), ())), preferred...  53.3 us
  transfers between devices with their start and end apart: 23, of which 17 were waited for; matrix products, arithmetic and copies ran while one was open for 7% of the time, Pallas kernels for 0%

commit v1 on v0

v1 whole, which is shorter than its diff:
```python
import functools
import math

import jax
import jax.numpy as jnp
from jax import lax
from jax.experimental import pallas as pl
from jax.experimental.pallas import tpu as pltpu
from jax.sharding import PartitionSpec as P

D_S = 1024
D_V = 256
H_V = 513
H_P = 640
D_E = 32
NEIGH = 30
D_MODEL = 512
HEADS = 8
HEAD_DIM = 64
CAP = 16
GROUP = 5
VMEM_LIMIT = 60 * 1024 * 1024

BF = jnp.bfloat16
F32 = jnp.float32


def layer_norm(values, gain_row):
    centred = values - jnp.mean(values, axis=-1, keepdims=True)
    spread = jnp.mean(centred * centred, axis=-1, keepdims=True)
    return centred * lax.rsqrt(spread + 1e-05) * gain_row


def vector_norm(vectors):
    mean_power = jnp.mean(jnp.sum(vectors * vectors, axis=0), axis=-1, keepdims=True)
    return vectors * lax.rsqrt(mean_power + 1e-05)[None]


def length_plus(vectors):
    return jnp.sqrt(jnp.sum(vectors * vectors, axis=0) + 1.0)


def vector_gate(vectors):
    return vectors * jax.nn.sigmoid(length_plus(vectors))[None]


def gelu_exact(values):
    return jax.nn.gelu(values, approximate=False)


def product(former, latter):
    return jnp.dot(former, latter, preferred_element_type=F32)


def product_lead(former, latter):
    leading = tuple(range(former.ndim - 1))
    return lax.dot_general(
        former, latter, ((leading, leading), ((), ())), preferred_element_type=F32
    )


def product_back(former, latter):
    return lax.dot_general(
        former, latter, (((former.ndim - 1,), (1,)), ((), ())), preferred_element_type=F32
    )


def pullback(function, at_point, cotangent_in):
    unused, puller = jax.vjp(function, at_point)
    return puller(cotangent_in)[0]


def sigmoid(values):
    return 0.5 * jnp.tanh(0.5 * values) + 0.5


LANE_BLOCKS = ((0, 256), (256, 256), (512, 128))
ROW_TILE = 64


def edge_forward_kernel(
    near_ref, es_ref, ev_ref, a_ref, b_ref, p_ref, q_ref, ve_ref, vo_ref,
    aggs_ref, aggv_ref, h_ref, lx_ref, ds_ref, z_ref, x_scr,
):
    nodes = b_ref.shape[0]
    table = p_ref.shape[1]
    rows = GROUP * nodes
    idx = near_ref[...].reshape(rows, 1)
    x_scr[:, :table] = (idx == lax.broadcasted_iota(jnp.int32, (rows, table), 1)).astype(BF)
    one_hot = x_scr[:, :table]
    for start, width in LANE_BLOCKS:
        cols = pl.ds(start, width)
        gathered = [product(one_hot, p_ref[c, :, cols]) for c in range(3)]
        for k in range(GROUP):
            for first in range(0, nodes, ROW_TILE):
                at = k * nodes + first
                evk = ev_ref[k, pl.ds(first, ROW_TILE), :]
                total = None
                for c in range(3):
                    h = (
                        gathered[c][at : at + ROW_TILE]
                        + q_ref[c, pl.ds(first, ROW_TILE), cols]
                        + evk[:, c : c + 1] * ve_ref[:, cols]
                    )
                    h_ref[k, c, pl.ds(first, ROW_TILE), cols] = h.astype(BF)
                    total = h * h + 1.0 if total is None else total + h * h
                length = total * lax.rsqrt(total)
                if start == 512:
                    lane = lax.broadcasted_iota(jnp.int32, (ROW_TILE, width), 1)
                    length = jnp.where(
                        lane == 0, length, es_ref[k, pl.ds(first, ROW_TILE), :].astype(F32)
                    )
                length = length.astype(BF)
                x_scr[pl.ds(at, ROW_TILE), pl.ds(table + start, width)] = length
                lx_ref[k, pl.ds(first, ROW_TILE), cols] = length

    @pl.when(pl.program_id(0) == 0)
    def _():
        aggs_ref[...] = jnp.zeros_like(aggs_ref)
        aggv_ref[...] = jnp.zeros_like(aggv_ref)

    full = x_scr[...]
    for start in range(0, D_S, 256):
        cols = pl.ds(start, 256)
        pre = product(full, a_ref[:, cols])
        for first in range(0, nodes, ROW_TILE):
            part = pl.ds(first, ROW_TILE)
            acc = None
            for k in range(GROUP):
                at = k * nodes + first
                x = pre[at : at + ROW_TILE] + b_ref[part, cols]
                s = sigmoid(x)
                y = x * s
                ds_ref[k, part, cols] = (s + y * (1.0 - s)).astype(BF)
                acc = y if acc is None else acc + y
            aggs_ref[part, cols] += acc * (1.0 / NEIGH)
    ups = [
        product(h_ref[:, c, :, :].reshape(rows, H_P), vo_ref[...]) for c in range(3)
    ]
    for first in range(0, nodes, ROW_TILE):
        part = pl.ds(first, ROW_TILE)
        acc = [None] * 3
        for k in range(GROUP):
            at = k * nodes + first
            z = [ups[c][at : at + ROW_TILE] for c in range(3)]
            power = z[0] * z[0] + z[1] * z[1] + z[2] * z[2] + 1.0
            s = sigmoid(power * lax.rsqrt(power))
            for c in range(3):
                z_ref[k, c, part, :] = z[c].astype(BF)
                gated = z[c] * s
                acc[c] = gated if acc[c] is None else acc[c] + gated
        for c in range(3):
            aggv_ref[c, part, :] += acc[c] * (1.0 / NEIGH)


def edge_forward(near_col, es_pad, ev_col, mix, b_target, p_source, q_target, ve_row, vout):
    nodes = b_target.shape[0]
    table = p_source.shape[1]
    whole = lambda shape: pl.BlockSpec(shape, lambda g: (0,) * len(shape))
    slots = lambda *shape: pl.BlockSpec((GROUP,) + shape, lambda g: (g,) + (0,) * len(shape))
    return pl.pallas_call(
        edge_forward_kernel,
        grid=(NEIGH // GROUP,),
        in_specs=[
            slots(nodes, 1),
            slots(nodes, 128),
            slots(nodes, 3),
            whole((table + H_P, D_S)),
            whole((nodes, D_S)),
            whole((3, table, H_P)),
            whole((3, nodes, H_P)),
            whole((1, H_P)),
            whole((H_P, D_V)),
        ],
        out_specs=[
            whole((nodes, D_S)),
            whole((3, nodes, D_V)),
            slots(3, nodes, H_P),
            slots(nodes, H_P),
            slots(nodes, D_S),
            slots(3, nodes, D_V),
        ],
        out_shape=[
            jax.ShapeDtypeStruct((nodes, D_S), F32),
            jax.ShapeDtypeStruct((3, nodes, D_V), F32),
            jax.ShapeDtypeStruct((NEIGH, 3, nodes, H_P), BF),
            jax.ShapeDtypeStruct((NEIGH, nodes, H_P), BF),
            jax.ShapeDtypeStruct((NEIGH, nodes, D_S), BF),
            jax.ShapeDtypeStruct((NEIGH, 3, nodes, D_V), BF),
        ],
        scratch_shapes=[pltpu.VMEM((GROUP * nodes, table + H_P), BF)],
        compiler_params=pltpu.CompilerParams(vmem_limit_bytes=VMEM_LIMIT),
        name="edge_forward",
    )(near_col, es_pad, ev_col, mix, b_target, p_source, q_target, ve_row, vout)


def edge_backward_kernel(
    near_ref, ev_ref, evr_ref, h_ref, lx_ref, ds_ref, z_ref, gs_ref, gv_ref, wn_ref, vo_ref,
    ga_ref, gw_ref, gb_ref, gp_ref, gq_ref, gvo_ref, pre_scr, up_scr, gh_scr,
):
    nodes = gs_ref.shape[0]
    table = ga_ref.shape[0]
    rows = GROUP * nodes

    @pl.when(pl.program_id(0) == 0)
    def _():
        for ref in (ga_ref, gw_ref, gb_ref, gp_ref, gq_ref, gvo_ref):
            ref[...] = jnp.zeros_like(ref)

    for start in range(0, D_S, 256):
        cols = pl.ds(start, 256)
        for first in range(0, nodes, ROW_TILE):
            part = pl.ds(first, ROW_TILE)
            share = gs_ref[part, cols]
            acc = None
            for k in range(GROUP):
                g = (ds_ref[k, part, cols].astype(F32) * share).astype(BF)
                pre_scr[pl.ds(k * nodes + first, ROW_TILE), cols] = g
                g = g.astype(F32)
                acc = g if acc is None else acc + g
            gb_ref[part, cols] += acc
    for first in range(0, nodes, ROW_TILE):
        part = pl.ds(first, ROW_TILE)
        share = [gv_ref[c, part, :] for c in range(3)]
        for k in range(GROUP):
            z = [z_ref[k, c, part, :].astype(F32) for c in range(3)]
            power = z[0] * z[0] + z[1] * z[1] + z[2] * z[2] + 1.0
            inverse = lax.rsqrt(power)
            s = sigmoid(power * inverse)
            dot = z[0] * share[0] + z[1] * share[1] + z[2] * share[2]
            factor = dot * inverse * (s * (1.0 - s))
            for c in range(3):
                up_scr[c, pl.ds(k * nodes + first, ROW_TILE), :] = (
                    share[c] * s + z[c] * factor
                ).astype(BF)

    near = near_ref[0]
    one_hot = (lax.broadcasted_iota(jnp.int32, (table, rows), 0) == near).astype(BF)
    grad_pre = pre_scr[...]
    ga_ref[...] += product(one_hot, grad_pre)
    lx = lx_ref[...].reshape(rows, H_P)
    gw_ref[...] += lax.dot_general(
        lx, grad_pre, (((0,), (0,)), ((), ())), preferred_element_type=F32
    )
    for start, width in LANE_BLOCKS:
        cols = pl.ds(start, width)
        grad_length = product_back(grad_pre, wn_ref[cols, :])
        grad_direct = [product_back(up_scr[c], vo_ref[cols, :]) for c in range(3)]
        for first in range(0, nodes, ROW_TILE):
            part = pl.ds(first, ROW_TILE)
            acc = [None] * 3
            for k in range(GROUP):
                at = k * nodes + first
                ratio = grad_length[at : at + ROW_TILE] * pl.reciprocal(
                    lx_ref[k, part, cols].astype(F32), approx=True
                )
                if start == 512:
                    lane = lax.broadcasted_iota(jnp.int32, (ROW_TILE, width), 1)
                    ratio = jnp.where(lane == 0, ratio, 0.0)
                for c in range(3):
                    g = grad_direct[c][at : at + ROW_TILE] + ratio * h_ref[
                        k, c, part, cols
                    ].astype(F32)
                    gh_scr[c, pl.ds(at, ROW_TILE), cols] = g.astype(BF)
                    acc[c] = g if acc[c] is None else acc[c] + g
            for c in range(3):
                gq_ref[c, part, cols] += acc[c]
    for c in range(3):
        evr = jnp.broadcast_to(evr_ref[0, c : c + 1, :], (16, rows))
        lead = jnp.concatenate([one_hot, evr.astype(BF)], axis=0)
        gp_ref[c] += product(lead, gh_scr[c])
        gvo_ref[...] += lax.dot_general(
            up_scr[c],
            h_ref[:, c, :, :].reshape(rows, H_P),
            (((0,), (0,)), ((), ())),
            preferred_element_type=F32,
        )


def edge_backward(near_row, ev_col, ev_row, hidden, lx, dsilu, update, gs, gv, wn, vout, table):
    nodes = gs.shape[0]
    rows = GROUP * nodes
    whole = lambda shape: pl.BlockSpec(shape, lambda g: (0,) * len(shape))
    slots = lambda *shape: pl.BlockSpec((GROUP,) + shape, lambda g: (g,) + (0,) * len(shape))
    steps = lambda *shape: pl.BlockSpec((1,) + shape, lambda g: (g,) + (0,) * len(shape))
    outs = [
        (table, D_S),
        (H_P, D_S),
        (nodes, D_S),
        (3, table + 16, H_P),
        (3, nodes, H_P),
        (D_V, H_P),
    ]
    return pl.pallas_call(
        edge_backward_kernel,
        grid=(NEIGH // GROUP,),
        in_specs=[
            steps(1, rows),
            slots(nodes, 3),
            steps(3, rows),
            slots(3, nodes, H_P),
            slots(nodes, H_P),
            slots(nodes, D_S),
            slots(3, nodes, D_V),
            whole((nodes, D_S)),
            whole((3, nodes, D_V)),
            whole((H_P, D_S)),
            whole((H_P, D_V)),
        ],
        out_specs=[whole(shape) for shape in outs],
        out_shape=[jax.ShapeDtypeStruct(shape, F32) for shape in outs],
        scratch_shapes=[
            pltpu.VMEM((rows, D_S), BF),
            pltpu.VMEM((3, rows, D_V), BF),
            pltpu.VMEM((3, rows, H_P), BF),
        ],
        compiler_params=pltpu.CompilerParams(vmem_limit_bytes=VMEM_LIMIT),
        name="edge_backward",
    )(near_row, ev_col, ev_row, hidden, lx, dsilu, update, gs, gv, wn, vout)


def pad_to(values, size, axis):
    pads = [(0, 0)] * values.ndim
    pads[axis] = (0, size - values.shape[axis])
    return jnp.pad(values, pads)


def fold(blocks, width=512):
    shards, rows, columns = blocks.shape
    parts = columns // width
    return jnp.moveaxis(blocks.reshape(shards, rows, parts, width), 2, 1).reshape(
        shards, parts * rows, width
    )


def unfold(rows_in, rows, columns, width=512):
    parts = columns // width
    return jnp.moveaxis(rows_in.reshape(parts, rows, width), 0, 1).reshape(rows, columns)


def body(
    node_scalar, node_vector, edge_scalar, edge_vector, neighbours, send_rows, complex_id, cotangent,
    w_node, w_edge, w_norms, vec_node, vec_edge, vec_out, norm_gain, ff_vec, ff_scalar, ff_up,
    w_embed, attn_gain, w_qkv, w_out, ffn_gain, w_up, w_down,
):
    local_rows = node_scalar.shape[0]
    spaces = lax.axis_size("space")
    extra_rows = spaces * CAP
    table_count = local_rows + extra_rows
    all_nodes = complex_id.shape[0]
    steps = NEIGH // GROUP

    sent_index = send_rows[0].reshape(-1)
    sent_live = sent_index >= 0
    pick = sent_index[:, None] == jnp.arange(local_rows, dtype=jnp.int32)[None, :]
    pick = pick.astype(BF)
    flat_nodes = jnp.concatenate([node_scalar] + [node_vector[c] for c in range(3)], 1)
    outgoing = product(pick, flat_nodes).astype(BF).reshape(spaces, CAP, D_S + 3 * D_V)
    incoming = lax.all_to_all(outgoing, "space", split_axis=0, concat_axis=0, tiled=True)
    incoming = incoming.reshape(extra_rows, D_S + 3 * D_V)
    table_s = jnp.concatenate([node_scalar, incoming[:, :D_S]], 0)
    table_v = jnp.stack(
        [
            jnp.concatenate(
                [node_vector[c], incoming[:, D_S + c * D_V : D_S + (c + 1) * D_V]], 0
            )
            for c in range(3)
        ]
    )
    vec_source = pad_to(vec_node[:, :H_V], H_P, 1)
    vec_target = pad_to(vec_node[:, H_V:], H_P, 1)
    a_source = product(table_s, w_node[:, :D_S]).astype(BF)
    b_target = product(node_scalar, w_node[:, D_S:])
    p_source = product(table_v, vec_source).astype(BF)
    q_target = product(node_vector, vec_target)
    ve_row = pad_to(vec_edge.astype(F32), H_P, 1)
    vout = pad_to(vec_out, H_P, 0)
    wn_mix = pad_to(jnp.concatenate([w_norms, w_edge], 0), H_P, 0)
    mix = jnp.concatenate([a_source, wn_mix], 0)

    near = neighbours.T
    near_col = near[:, :, None]
    near_row = near.reshape(steps, 1, GROUP * local_rows)
    es_k = edge_scalar.reshape(local_rows, NEIGH, D_E).transpose(1, 0, 2)
    es_pad = jnp.pad(es_k, ((0, 0), (0, 0), (1, 128 - 1 - D_E)))
    ev_k = edge_vector.reshape(3, local_rows, NEIGH)
    ev_col = ev_k.transpose(2, 1, 0).astype(F32)
    ev_row = ev_k.transpose(2, 0, 1).reshape(steps, GROUP, 3, local_rows)
    ev_row = ev_row.transpose(0, 2, 1, 3).reshape(steps, 3, GROUP * local_rows)

    agg_s, agg_v, hidden, lx, dsilu, update = edge_forward(
        near_col, es_pad, ev_col, mix, b_target, p_source, q_target, ve_row, vout
    )

    scalar_one = node_scalar.astype(F32) + agg_s
    vector_one = node_vector.astype(F32) + agg_v
    gain_norm = norm_gain.astype(F32)
    normed_s = layer_norm(scalar_one, gain_norm)
    normed_v = vector_norm(vector_one)
    normed_vr = normed_v.astype(BF)
    ff_hidden = product(normed_vr, ff_vec)
    ff_hidden_r = ff_hidden.astype(BF)
    ff_length = length_plus(ff_hidden)
    ff_input = jnp.concatenate([normed_s.astype(BF), ff_length.astype(BF)], -1)
    ff_preact = product(ff_input, ff_scalar)
    ff_update = product(ff_hidden_r, ff_up)
    scalar_two = normed_s + jax.nn.silu(ff_preact)
    vector_two = normed_v + vector_gate(ff_update)
    embed_input = jnp.concatenate([scalar_two.astype(BF), length_plus(vector_two).astype(BF)], -1)
    stream_zero = product(embed_input, w_embed)
    gain_attn = attn_gain.astype(F32)
    attn_in = layer_norm(stream_zero, gain_attn).astype(BF)
    qkv = product(attn_in, w_qkv).astype(BF)
    queries = qkv[:, :D_MODEL]
    keys_own = qkv[:, D_MODEL : 2 * D_MODEL]
    values_own = qkv[:, 2 * D_MODEL :]
    full_qkv = lax.all_gather(qkv, "space", axis=0, tiled=True)
    heads = lambda values: values.reshape(values.shape[0], HEADS, HEAD_DIM)
    full_queries = heads(full_qkv[:, :D_MODEL])
    full_keys = heads(full_qkv[:, D_MODEL : 2 * D_MODEL])
    full_values = heads(full_qkv[:, 2 * D_MODEL :])
    position = lax.axis_index("space")
    own_ids = lax.dynamic_slice_in_dim(complex_id, position * local_rows, local_rows, 0)
    same = own_ids[:, None] == complex_id[None, :]
    score_scale = HEAD_DIM ** (-0.5)
    scores = jnp.einsum("qhd,khd->hqk", heads(queries), full_keys, preferred_element_type=F32)
    scores = jnp.where(same[None], scores * score_scale, -1000000000.0)
    row_peak = jnp.max(scores, axis=-1, keepdims=True)
    shifted = jnp.exp(scores - row_peak)
    totals = jnp.sum(shifted, axis=-1, keepdims=True)
    probs = shifted / totals
    log_total = row_peak + jnp.log(totals)
    attended = jnp.einsum(
        "hqk,khd->qhd", probs.astype(BF), full_values, preferred_element_type=F32
    ).reshape(local_rows, D_MODEL)
    attended_r = attended.astype(BF)
    stream_one = stream_zero + product(attended_r, w_out)
    gain_ffn = ffn_gain.astype(F32)
    ffn_in = layer_norm(stream_one, gain_ffn).astype(BF)
    hidden_up = product(ffn_in, w_up)
    gelu_r = gelu_exact(hidden_up).astype(BF)
    stream_out = (stream_one + product(gelu_r, w_down)).astype(BF)
    grad_w_down = product_lead(gelu_r, cotangent)
    grad_gelu = product_back(cotangent, w_down)
    grad_up_r = pullback(gelu_exact, hidden_up, grad_gelu).astype(BF)
    grad_w_up = product_lead(ffn_in, grad_up_r)
    grad_ffn_in = product_back(grad_up_r, w_up)
    unused, ffn_pull = jax.vjp(layer_norm, stream_one, gain_ffn)
    grad_stream_ln, grad_ffn_gain = ffn_pull(grad_ffn_in)
    grad_stream_one = cotangent.astype(F32) + grad_stream_ln
    grad_branch = grad_stream_one.astype(BF)
    grad_w_out = product_lead(attended_r, grad_branch)
    grad_attended = product_back(grad_branch, w_out).astype(BF)
    row_dots = jnp.sum(heads(grad_attended).astype(F32) * heads(attended), axis=-1).T

    def halves(values):
        high = lax.reduce_precision(values, exponent_bits=8, mantissa_bits=7)
        return [high.astype(BF), (values - high).astype(BF)]

    numbers = jnp.concatenate(halves(log_total[:, :, 0]) + halves(row_dots), 0)
    packed = jnp.concatenate([grad_attended, pad_to(numbers.T, 128, 1)], 1)
    full_packed = lax.all_gather(packed, "space", axis=0, tiled=True)
    full_grad = heads(full_packed[:, :D_MODEL])
    numbers = full_packed[:, D_MODEL : D_MODEL + 4 * HEADS].astype(F32).T
    full_log = numbers[:HEADS] + numbers[HEADS : 2 * HEADS]
    full_dots = numbers[2 * HEADS : 3 * HEADS] + numbers[3 * HEADS :]

    grad_probs = jnp.einsum(
        "qhd,khd->hqk", heads(grad_attended), full_values, preferred_element_type=F32
    )
    grad_scores = (probs * (grad_probs - row_dots[:, :, None])).astype(BF)
    grad_query = jnp.einsum("hqk,khd->qhd", grad_scores, full_keys, preferred_element_type=F32)
    own_scores = jnp.einsum(
        "khd,qhd->hkq", heads(keys_own), full_queries, preferred_element_type=F32
    )
    own_scores = jnp.where(same[None], own_scores * score_scale, -1000000000.0)
    own_probs = jnp.exp(own_scores - full_log[:, None, :])
    own_grad_probs = jnp.einsum(
        "khd,qhd->hkq", heads(values_own), full_grad, preferred_element_type=F32
    )
    own_grad_scores = (own_probs * (own_grad_probs - full_dots[:, None, :])).astype(BF)
    grad_keys = jnp.einsum(
        "hkq,qhd->khd", own_grad_scores, full_queries, preferred_element_type=F32
    )
    grad_values = jnp.einsum(
        "hkq,qhd->khd", own_probs.astype(BF), full_grad, preferred_element_type=F32
    )
    flat = lambda values: values.reshape(local_rows, D_MODEL)
    grad_qkv = jnp.concatenate(
        [flat(grad_query) * score_scale, flat(grad_keys) * score_scale, flat(grad_values)], -1
    ).astype(BF)
    grad_w_qkv = product_lead(attn_in, grad_qkv)
    grad_attn_in = product_back(grad_qkv, w_qkv)
    unused, attn_pull = jax.vjp(layer_norm, stream_zero, gain_attn)
    grad_zero_ln, grad_attn_gain = attn_pull(grad_attn_in)
    grad_stream_r = (grad_stream_one + grad_zero_ln).astype(BF)
    grad_w_embed = product_lead(embed_input, grad_stream_r)
    grad_embed_in = product_back(grad_stream_r, w_embed)
    grad_vector_two = pullback(length_plus, vector_two, grad_embed_in[:, D_S:])
    grad_ff_pre = pullback(jax.nn.silu, ff_preact, grad_embed_in[:, :D_S]).astype(BF)
    grad_ff_scalar = product_lead(ff_input, grad_ff_pre)
    grad_ff_input = product_back(grad_ff_pre, ff_scalar)
    grad_ff_update = pullback(vector_gate, ff_update, grad_vector_two).astype(BF)
    grad_ff_up = product_lead(ff_hidden_r, grad_ff_update)
    grad_ff_hidden = (
        product_back(grad_ff_update, ff_up)
        + pullback(length_plus, ff_hidden, grad_ff_input[:, D_S:])
    ).astype(BF)
    grad_ff_vec = product_lead(normed_vr, grad_ff_hidden)
    grad_normed_v = grad_vector_two + product_back(grad_ff_hidden, ff_vec)
    grad_normed_s = grad_embed_in[:, :D_S] + grad_ff_input[:, :D_S]
    unused, norm_pull = jax.vjp(layer_norm, scalar_one, gain_norm)
    grad_scalar_one, grad_norm_gain = norm_pull(grad_normed_s)
    grad_vector_one = pullback(vector_norm, vector_one, grad_normed_v)

    shard = lambda grad: grad.astype(BF).reshape((spaces, grad.shape[0] // spaces) + grad.shape[1:])
    gains = jnp.concatenate(
        [shard(grad_norm_gain), shard(grad_attn_gain), shard(grad_ffn_gain)], 1
    )
    gains = pad_to(pad_to(gains, 512, 1)[:, None, :], 16, 1)
    first_share = jnp.concatenate(
        [
            shard(grad_w_down),
            fold(shard(grad_w_up)),
            fold(shard(grad_w_qkv)),
            shard(grad_w_out),
            shard(grad_w_embed),
            fold(shard(grad_ff_scalar)),
            jnp.concatenate([shard(grad_ff_vec), shard(grad_ff_up)], 2),
            gains,
        ],
        1,
    )
    first_sum = lax.psum_scatter(first_share, "space", scatter_dimension=0, tiled=False)
    first_sum = lax.psum(first_sum, "dp").astype(F32)

    grad_a, grad_mix, grad_b, grad_p, grad_q, grad_vout = edge_backward(
        near_row, ev_col, ev_row, hidden, lx, dsilu, update,
        grad_scalar_one * (1.0 / NEIGH), grad_vector_one * (1.0 / NEIGH), wn_mix, vout, table_count,
    )
    grad_vedge = jnp.sum(grad_p[:, table_count], 0)[:H_V]
    grad_vec_edge = lax.psum(grad_vedge[None, :], ("dp", "space"))
    grad_a_r = grad_a.astype(BF)
    grad_p_r = grad_p[:, :table_count].astype(BF)
    grad_b_r = grad_b.astype(BF)
    grad_q_r = grad_q.astype(BF)
    grad_node_a = product_lead(table_s, grad_a_r)
    grad_node_b = product_lead(node_scalar, grad_b_r)
    grad_vec_a = product_lead(table_v, grad_p_r)
    grad_vec_b = product_lead(node_vector, grad_q_r)
    grad_table_scalar = product_back(grad_a_r, w_node[:, :D_S])
    grad_table_vector = product_back(grad_p_r, vec_source)
    grad_scalar = (
        grad_scalar_one + product_back(grad_b_r, w_node[:, D_S:]) + grad_table_scalar[:local_rows]
    )
    grad_vector = (
        grad_vector_one + product_back(grad_q_r, vec_target) + grad_table_vector[:, :local_rows]
    )
    back = jnp.concatenate(
        [grad_table_scalar[local_rows:]] + [grad_table_vector[c, local_rows:] for c in range(3)], 1
    )
    back = back.astype(BF).reshape(spaces, CAP, D_S + 3 * D_V)
    got = lax.all_to_all(back, "space", split_axis=0, concat_axis=0, tiled=True)
    got = got.reshape(extra_rows, D_S + 3 * D_V)
    got = jnp.where(sent_live[:, None], got, 0)
    added = lax.dot_general(pick, got, (((0,), (0,)), ((), ())), preferred_element_type=F32)
    grad_scalar = grad_scalar + added[:, :D_S]
    grad_vector = grad_vector + jnp.moveaxis(
        added[:, D_S:].reshape(local_rows, 3, D_V), 1, 0
    )

    columns = lambda grad: jnp.moveaxis(
        grad.reshape(grad.shape[0], spaces, grad.shape[1] // spaces), 1, 0
    )
    mix_block = columns(grad_mix.astype(BF))
    mix_width = D_S // spaces
    mix_rows = H_P * mix_width // 512
    second_share = jnp.concatenate(
        [
            fold(shard(grad_node_a)),
            fold(shard(grad_node_b)),
            mix_block.reshape(spaces, mix_rows, 512),
            shard(grad_vec_a)[:, :, :512],
            shard(grad_vec_b)[:, :, :512],
            shard(grad_vout)[:, :, :512],
            jnp.concatenate(
                [
                    shard(grad_vec_a)[:, :, 512:],
                    shard(grad_vec_b)[:, :, 512:],
                    shard(grad_vout)[:, :, 512:],
                    jnp.zeros((spaces, D_V // spaces, 128), BF),
                ],
                2,
            ),
        ],
        1,
    )
    second_sum = lax.psum_scatter(second_share, "space", scatter_dimension=0, tiled=False)
    second_sum = lax.psum(second_sum, "dp").astype(F32)

    def taker(rows_in):
        at = [0]

        def take(rows, cols, blocks=1):
            part = rows_in[at[0] : at[0] + rows * blocks]
            at[0] += rows * blocks
            return unfold(part, rows, cols) if blocks > 1 else part

        return take

    take = taker(first_sum)
    out_down = take(grad_w_down.shape[0] // spaces, 512)
    out_up = take(D_MODEL // spaces, 2048, 4)
    out_qkv = take(D_MODEL // spaces, 1536, 3)
    out_out = take(D_MODEL // spaces, 512)
    out_embed = take((D_S + D_V) // spaces, 512)
    out_ffs = take((D_S + D_V) // spaces, 1024, 2)
    both = take(D_V // spaces, 512)
    out_ffv, out_ffu = both[:, :D_V], both[:, D_V:]
    gain_row = take(16, 512)[0]
    cuts = [D_S // spaces, D_MODEL // spaces, D_MODEL // spaces]
    out_gn = gain_row[: cuts[0]]
    out_ga = gain_row[cuts[0] : cuts[0] + cuts[1]]
    out_gf = gain_row[cuts[0] + cuts[1] : sum(cuts)]
    take = taker(second_sum)
    node_a = take(D_S // spaces, 1024, 2)
    node_b = take(D_S // spaces, 1024, 2)
    mixed = take(mix_rows, 512).reshape(H_P, mix_width)
    vec_a = take(D_V // spaces, 512)
    vec_b = take(D_V // spaces, 512)
    vout_t = take(D_V // spaces, 512)
    tails = take(D_V // spaces, 512)
    out_vec_node = jnp.concatenate([vec_a, tails[:, :1], vec_b, tails[:, 128:129]], 1)
    out_vec_out = jnp.concatenate([vout_t, tails[:, 256:257]], 1).T
    return (
        stream_out,
        grad_scalar.astype(BF),
        grad_vector.astype(BF),
        jnp.concatenate([node_a, node_b], 1),
        mixed[H_V : H_V + D_E],
        mixed[:H_V],
        out_vec_node,
        grad_vec_edge,
        out_vec_out,
        out_gn,
        out_ffv,
        out_ffs,
        out_ffu,
        out_embed,
        out_ga,
        out_qkv,
        out_out,
        out_gf,
        out_up,
        out_down,
    )


def solution(mesh):
    rows = P(("dp", "space"), None)
    component = P(None, ("dp", "space"), None)
    return jax.shard_map(
        body,
        mesh=mesh,
        in_specs=(
            rows, component, rows, P(None, ("dp", "space")), rows,
            P(("dp", "space"), None, None), P("dp"), rows,
        ) + (P(),) * 17,
        out_specs=(
            rows, rows, component, P("space", None), P(None, "space"), P(None, "space"),
            P("space", None), P(), P(None, "space"), P("space"), P("space", None),
            P("space", None), P("space", None), P("space", None), P("space"), P("space", None),
            P("space", None), P("space"), P("space", None), P("space", None),
        ),
        check_vma=False,
    )
```

time: 2150 us -> 591 us (0.27)
  other arithmetic: 707 us -> 32.1 us
  waiting for transfers between devices: 612 us -> 194 us
  local copies, waits for them, and re-layouts: 464 us -> 130 us
  matrix products: 229 us -> 78.6 us
  Pallas kernels: 0 us -> 79.9 us
  loops' own time: 32 us -> 0 us
    scatter-add x10 -> x0, other arithmetic: 558 us -> none  [the longest x4 507 us: edge_back(): grad_p = grad_p.at[:, flat_nearby].add(grad_hidden.reshape(3, -1, H_V))]
    reduce_scatter x14 -> x2, waiting for transfers between devices: 504 us -> 141 us  [the longest x1 113 us: body(): lax.psum_scatter(first_share, 'space', scatter_dimension=0, tiled=False)]
    gather x27 -> x0, local copies, waits for them, and re-layouts: 227 us -> none  [the longest x8 136 us: edge_forward(): p_source[:, nearby] + target_q[:, :, None]]
    reshape x39 -> x15, local copies, waits for them, and re-layouts: 107 us -> 13.5 us  [the longest x2 2.79 us: body(): ev_row = ev_row.transpose(0, 2, 1, 3).reshape(steps, 3, GROUP * local_rows)]
    dot_general x46 -> x20, matrix products: 128 us -> 42.4 us  [the longest x13 18.1 us: product(): return jnp.dot(former, latter, preferred_element_type=F32)]
    pallas_call x0 -> x2, Pallas kernels: none -> 79.9 us  [the longest x1 44.5 us: edge_backward(): pl.pallas_call(edge_backward_kernel, grid=(NEIGH // GROUP,), in_specs=[st...]
    convert_element_type x52 -> x15, other arithmetic: 76.3 us -> 5.38 us  [the longest x1 1.12 us: body(): grad.astype(BF).reshape((spaces, grad.shape[0] // spaces) + grad.shape[1:])]
    dot_general x24 -> x12, matrix products: 53.3 us -> 14.8 us  [product_lead(): lax.dot_general(former, latter, ((leading, leading), ((), ())), preferred...]
  transfers between devices with their start and end apart: 23 -> 7, of which waited for: 17 -> 4; matrix products, arithmetic and copies ran while one was open for 7% -> 18% of each run, Pallas kernels for 0% -> 0%
where the time goes in v1:
time: 591 us; the launch traced here: 581 us
  waiting for transfers between devices  194 us (33%)
  local copies, waits for them, and re-layouts  130 us (22%)
  Pallas kernels  79.9 us (14%)
  matrix products  78.6 us (13%)
  blocking collectives  38.3 us (6%)
  other arithmetic  32.1 us (5%)
  between operations  16.2 us (3%)
  starting transfers between devices  11.6 us (2%)
    reduce_scatter x1, waiting for transfers between devices, body(): lax.psum_scatter(first_share, 'space', scatter_dimension=0, tiled=False)  113 us
    pallas_call x1, Pallas kernels, edge_backward(): pl.pallas_call(edge_backward_kernel, grid=(NEIGH // GROUP,), in_specs=[st...  44.5 us
    psum x1, blocking collectives, body(): grad_vec_edge = lax.psum(grad_vedge[None, :], ('dp', 'space'))  38.3 us
    pallas_call x1, Pallas kernels, edge_forward(): pl.pallas_call(edge_forward_kernel, grid=(NEIGH // GROUP,), in_specs=[slo...  35.4 us
    all_gather x1, waiting for transfers between devices, body(): full_qkv = lax.all_gather(qkv, 'space', axis=0, tiled=True)  32.9 us
    reduce_scatter x1, waiting for transfers between devices, body(): lax.psum_scatter(second_share, 'space', scatter_dimension=0, tiled=False)  28.6 us
    unnamed x316, local copies, waits for them, and re-layouts  28 us
    dot_general x12, matrix products, product_back(): lax.dot_general(former, latter, (((former.ndim - 1,), (1,)), ((), ())), p...  21.4 us
  transfers between devices with their start and end apart: 7, of which 4 were waited for; matrix products, arithmetic and copies ran while one was open for 18% of the time, Pallas kernels for 0%

profile of v1, /device:TPU:0, one launch (start us, length us, event | category | flops | bytes accessed | tf_op | source)
XLA Modules:
  0.0 580.7 jit_solution(14508295174438755802)
XLA Ops:
  11.8 6.3 %all-to-all-start = ((bf16[8,16,1792]{2,1,0:T(8,128)(2,1)}), bf16[8,16,1792]{2,1,0:T(8,128)(2,1)}, u32[]{:S(2)}, u32[]{:S(2)}) async-start(bf16[8,16,1792]{2,1,0:T(8,128)(2,1)} %bitcast.8), calls=%async_computation | async-start | bytes 917504 | tf_op jit(solution)/shard_map/all_to_all | solution.py:359
  23.8 2.5 pad.37.es_ref
  27.9 2.6 copy.201.near_ref
  31.1 2.5 fusion.21.wn_ref
  34.9 2.9 fusion.13.b_ref
  45.4 35.4 %edge_forward.1 = (f32[128,1024]{1,0:T(8,128)}, f32[3,128,256]{2,1,0:T(8,128)}, bf16[30,3,128,640]{3,2,1,0:T(8,128)(2,1)}, bf16[30,128,640]{2,1,0:T(8,128)(2,1)}...) custom-call(s32[30,128,1]{2,1,0:T(8,128)} %copy.201.near_ref, bf16[30,128,128]{2,1,0:T(8,128)(2,1)} %pad.37.es_ref, ...), custom_call_target="tpu_custom_call" | custom-call | tf_op jit(solution)/shard_map/edge_forward/pallas_call | solution.py:161
  98.9 32.9 %all-gather.3.cloned.1.call-done = bf16[1024,1536]{1,0:T(8,128)(2,1)} async-done(((bf16[128,1536]{1,0:T(8,128)(2,1)}), bf16[1024,1536]{1,0:T(8,128)(2,1)}) %all-gather.3.cloned.1.call-update) | async-done | bytes 3145744 | tf_op jit(solution)/shard_map/all_gather | solution.py:417
  131.8 3.6 fusion.150
  148.1 3.8 add_convert_fusion
  177.1 4.0 fusion.163
  181.1 5.7 fusion.50
  197.4 4.3 fusion.53
  201.7 5.6 fusion.48
  207.4 3.0 multiply_reduce_fusion.10
  218.3 44.5 %edge_backward.1 = (f32[256,1024]{1,0:T(8,128)}, f32[640,1024]{1,0:T(8,128)}, f32[128,1024]{1,0:T(8,128)}, f32[3,272,640]{2,1,0:T(8,128)}, f32[3,128,640]{2,1,0:T(8,128)}, /*index=5*/f32[256,640]{1,0:T(8,128)}) custom-call(s32[6,1,640]{2,1,0:T(1,128)} %reshape.383.near_ref, f32[30,128,3]{2,1,0:T(8,128)} %bitcast.231, bf16[6,3,640]{2,1,0:T(4,128)(2,1)} %copy.214.evr_ref, ...), custom_call_target="tpu_custom_call" | custom-call | tf_op jit(solution)/shard_map/edge_backward/pallas_call | solution.py:294
  262.9 2.9 fusion.35
  274.0 2.8 reshape_reshape.15
  281.5 4.3 copy.220
  295.8 2.8 reshape_reshape.17
  298.5 2.4 copy.226
  306.2 2.9 convolution_convert_fusion.3
  309.2 4.6 reshape_reshape.18
  317.9 5.5 reshape_reshape.19
  333.5 2.9 fusion.15
  339.8 4.1 all-to-all-start.1
  343.9 28.6 %reduce-scatter.3.cloned.1.call-done = bf16[1,800,512]{2,1,0:T(8,128)(2,1)} async-done(((bf16[8,800,512]{2,1,0:T(8,128)(2,1)}), bf16[1,800,512]{2,1,0:T(8,128)(2,1)}) %reduce-scatter.3.cloned.1.call-update) | async-done | bytes 819216 | tf_op jit(solution)/shard_map/reduce_scatter | solution.py:598
  372.6 112.7 %reduce-scatter.5.cloned.1.call-done = bf16[1,1296,512]{2,1,0:T(8,128)(2,1)} async-done(((bf16[8,1296,512]{2,1,0:T(8,128)(2,1)}), bf16[1,1296,512]{2,1,0:T(8,128)(2,1)}) %reduce-scatter.5.cloned.1.call-update) | async-done | bytes 1327120 | tf_op jit(solution)/shard_map/reduce_scatter | solution.py:534
  485.4 2.7 fusion.49
  488.1 38.3 %psum.22 = f32[1,513]{1,0:T(1,128)} all-reduce(f32[1,513]{1,0:T(1,128)S(1)} %broadcast_in_dim.122), channel_id=1, replica_groups=mesh['dp'=4,'space'=8] {'dp','space'}, use_global_device_ids=true, to_apply=%region_24.25 | all-reduce | flops 513 | bytes 4104 | tf_op jit(solution)/shard_map/psum | solution.py:542
  532.6 2.5 fusion.41
  535.2 3.1 fusion.36
  538.3 19.8 %all-reduce.11.cloned.1.call-done = (bf16[800,512]{1,0:T(8,128)(2,1)}, bf16[1296,512]{1,0:T(8,128)(2,1)}) async-done(((bf16[800,512]{1,0:T(8,128)(2,1)}, bf16[1296,512]{1,0:T(8,128)(2,1)}), (bf16[800,512]{1,0:T(8,128)(2,1)}, bf16[1296,512]{1,0:T(8,128)(2,1)})) %all-reduce.11.cloned.1.call-update) | async-done | bytes 2146320 | tf_op jit(solution)/shard_map/psum | solution.py:599
  (496 shorter events, 161.8 us)
Async XLA Ops:
  7.2 80.6 %copy-start = (bf16[1280,1024]{1,0:T(8,128)(2,1)S(1)}, bf16[1280,1024]{1,0:T(8,128)(2,1)}, u32[]{:S(2)}) copy-start(bf16[1280,1024]{1,0:T(8,128)(2,1)} %param.41) | copy-start | bytes 7864324
  7.2 14.5 %copy-start.112 = (bf16[128,960]{0,1:T(8,128)(2,1)S(1)}, bf16[128,960]{0,1:T(8,128)(2,1)}, u32[]{:S(2)}) copy-start(bf16[128,960]{0,1:T(8,128)(2,1)} %param.27) | copy-start | bytes 737284
  7.2 15.8 %copy-start.102 = (bf16[513,256]{1,0:T(8,128)(2,1)S(1)}, bf16[513,256]{1,0:T(8,128)(2,1)}, u32[]{:S(2)}) copy-start(bf16[513,256]{1,0:T(8,128)(2,1)} %param.38) | copy-start | bytes 787972
  8.1 11.4 %copy-start.134 = (s32[128]{0:T(128)}, s32[128]{0:T(128)S(1)}, u32[]{:S(2)}) copy-start(s32[128]{0:T(128)S(1)} %eq.32) | copy-start | bytes 1540
  9.1 9.7 %copy-start.106 = (bf16[128,256]{1,0:T(8,128)(2,1)}, bf16[128,256]{1,0:T(8,128)(2,1)S(1)}, u32[]{:S(2)}) copy-start(bf16[128,256]{1,0:T(8,128)(2,1)S(1)} %get-tuple-element.93) | copy-start | bytes 196612
  11.8 26.0 %all-to-all-start = ((bf16[8,16,1792]{2,1,0:T(8,128)(2,1)}), bf16[8,16,1792]{2,1,0:T(8,128)(2,1)}, u32[]{:S(2)}, u32[]{:S(2)}) async-start(bf16[8,16,1792]{2,1,0:T(8,128)(2,1)} %bitcast.8), calls=%async_computation | async-start | bytes 917504 | tf_op jit(solution)/shard_map/all_to_all | solution.py:359
  18.1 113.7 %all-gather.3.cloned.1.call-start = ((), (), s32[]{:S(2)}) async-start(), calls=%async_computation.4 | async-start | bytes 3538944 | tf_op jit(solution)/shard_map/all_gather | solution.py:417
  18.9 192.2 %copy-start.114 = (f32[512]{0:T(512)}, f32[512]{0:T(512)S(1)}, u32[]{:S(2)}) copy-start(f32[512]{0:T(512)S(1)} %convert_element_type.252) | copy-start | bytes 6148
  21.7 11.9 %copy-start.39 = (bf16[256,513]{0,1:T(8,128)(2,1)}, bf16[256,513]{0,1:T(8,128)(2,1)S(1)}, u32[]{:S(2)}) copy-start(bf16[256,513]{0,1:T(8,128)(2,1)S(1)} %slice.242) | copy-start | bytes 787972
  23.0 7.6 %copy-start.133 = (bf16[1,513]{1,0:T(2,128)(2,1)S(1)}, bf16[1,513]{1,0:T(2,128)(2,1)}, u32[]{:S(2)}) copy-start(bf16[1,513]{1,0:T(2,128)(2,1)} %param.37) | copy-start | bytes 3082
  23.8 7.4 %copy-start.113 = (bf16[32,1024]{1,0:T(8,128)(2,1)S(1)}, bf16[32,1024]{1,0:T(8,128)(2,1)}, u32[]{:S(2)}) copy-start(bf16[32,1024]{1,0:T(8,128)(2,1)} %param.34) | copy-start | bytes 196612
  45.3 35.4 %copy-start.41 = (bf16[128,1024]{1,0:T(8,128)(2,1)S(1)}, bf16[128,1024]{1,0:T(8,128)(2,1)}, u32[]{:S(2)}) copy-start(bf16[128,1024]{1,0:T(8,128)(2,1)} %param.25) | copy-start | bytes 786436
  45.3 36.9 %copy-start.36 = (bf16[3,128,256]{2,1,0:T(8,128)(2,1)S(1)}, bf16[3,128,256]{2,1,0:T(8,128)(2,1)}, u32[]{:S(2)}) copy-start(bf16[3,128,256]{2,1,0:T(8,128)(2,1)} %param.26) | copy-start | bytes 589828
  90.7 44.7 %copy-start.130 = (f32[128]{0:T(128)}, f32[128]{0:T(128)S(1)}, u32[]{:S(2)}) copy-start(f32[128]{0:T(128)S(1)} %fusion.119) | copy-start | bytes 1540
  91.9 94.9 %all-gather.5.cloned.1.call-start = ((), (), s32[]{:S(2)}) async-start(), calls=%async_computation.5 | async-start | bytes 1474560 | tf_op jit(solution)/shard_map/all_gather | solution.py:462
  163.6 209.0 %reduce-scatter.3.cloned.1.call-start = ((), (), s32[]{:S(2)}) async-start(), calls=%async_computation.6 | async-start | bytes 7372800 | tf_op jit(solution)/shard_map/reduce_scatter | solution.py:598
  215.7 47.1 %copy-start.56 = (bf16[3,128,256]{2,1,0:T(8,128)(2,1)}, bf16[3,128,256]{2,1,0:T(8,128)(2,1)S(1)}, u32[]{:S(2)}) copy-start(bf16[3,128,256]{2,1,0:T(8,128)(2,1)S(1)} %fusion.42) | copy-start | bytes 589828
  216.0 46.8 %copy-start.28 = (f32[3,128,256]{2,1,0:T(8,128)}, f32[3,128,256]{2,1,0:T(8,128)S(1)}, u32[]{:S(2)}) copy-start(f32[3,128,256]{2,1,0:T(8,128)S(1)} %get-tuple-element.116) | copy-start | bytes 1179652
  216.4 46.4 %copy-start.22 = (f32[128,1024]{1,0:T(8,128)}, f32[128,1024]{1,0:T(8,128)S(1)}, u32[]{:S(2)}) copy-start(f32[128,1024]{1,0:T(8,128)S(1)} %get-tuple-element.53) | copy-start | bytes 1572868
  216.4 46.4 %copy-start.136 = (f32[128]{0:T(128)}, f32[128]{0:T(128)S(1)}, u32[]{:S(2)}) copy-start(f32[128]{0:T(128)S(1)} %negate_multiply_fusion.1) | copy-start | bytes 1540
  218.2 44.6 %copy-start.97 = (bf16[1,256,256]{2,1,0:T(8,128)(2,1)S(1)}, bf16[1,256,256]{2,1,0:T(8,128)(2,1)}, u32[]{:S(2)}) copy-start(bf16[1,256,256]{2,1,0:T(8,128)(2,1)} %copy-done.96) | copy-start | bytes 393220
  218.2 44.6 %copy-start.99 = (bf16[1,256,256]{2,1,0:T(8,128)(2,1)S(1)}, bf16[1,256,256]{2,1,0:T(8,128)(2,1)}, u32[]{:S(2)}) copy-start(bf16[1,256,256]{2,1,0:T(8,128)(2,1)} %copy-done.98) | copy-start | bytes 393220
  218.3 44.6 %copy-start.101 = (bf16[1,256,256]{2,1,0:T(8,128)(2,1)S(1)}, bf16[1,256,256]{2,1,0:T(8,128)(2,1)}, u32[]{:S(2)}) copy-start(bf16[1,256,256]{2,1,0:T(8,128)(2,1)} %copy-done.100) | copy-start | bytes 393220
  293.9 191.4 %reduce-scatter.5.cloned.1.call-start = ((), (), s32[]{:S(2)}) async-start(), calls=%async_computation.7 | async-start | bytes 11943936 | tf_op jit(solution)/shard_map/reduce_scatter | solution.py:534
  337.4 147.9 %copy-start.135 = (s32[128]{0:T(128)S(1)}, s32[128]{0:T(128)}, u32[]{:S(2)}) copy-start(s32[128]{0:T(128)} %copy-done.134) | copy-start | bytes 1540
  339.8 186.6 %all-to-all-start.1 = ((bf16[8,16,1792]{2,1,0:T(8,128)(2,1)}), bf16[8,16,1792]{2,1,0:T(8,128)(2,1)}, u32[]{:S(2)}, u32[]{:S(2)}) async-start(bf16[8,16,1792]{2,1,0:T(8,128)(2,1)} %pad_maximum_fusion.3), calls=%async_computation.1 | async-start | bytes 917504 | tf_op jit(solution)/shard_map/all_to_all | solution.py:563
  343.9 214.2 %all-reduce.11.cloned.1.call-start = ((), (), s32[]{:S(2)}) async-start(), calls=%async_computation.8 | async-start | bytes 4292608 | tf_op jit(solution)/shard_map/psum | solution.py:599
  485.3 47.3 %copy-start.141 = (f32[128]{0:T(128)S(1)}, f32[128]{0:T(128)}, u32[]{:S(2)}) copy-start(f32[128]{0:T(128)} %copy-done.140) | copy-start | bytes 1540
  488.1 44.5 %copy-start.29 = (f32[3,128,256]{2,1,0:T(8,128)S(1)}, f32[3,128,256]{2,1,0:T(8,128)}, u32[]{:S(2)}) copy-start(f32[3,128,256]{2,1,0:T(8,128)} %copy-done.28) | copy-start | bytes 1179652
  527.5 7.6 %copy-start.23 = (f32[128,1024]{1,0:T(8,128)S(1)}, f32[128,1024]{1,0:T(8,128)}, u32[]{:S(2)}) copy-start(f32[128,1024]{1,0:T(8,128)} %copy-done.22) | copy-start | bytes 1572868
  527.6 7.6 %copy-start.34 = (f32[256,1024]{1,0:T(8,128)S(1)}, f32[256,1024]{1,0:T(8,128)}, u32[]{:S(2)}) copy-start(f32[256,1024]{1,0:T(8,128)} %copy-done.33) | copy-start | bytes 3145732
  527.6 7.6 %copy-start.137 = (f32[128]{0:T(128)S(1)}, f32[128]{0:T(128)}, u32[]{:S(2)}) copy-start(f32[128]{0:T(128)} %copy-done.136) | copy-start | bytes 1540
  (125 other events, 358.4 us)
Sparse Core Ops, SparseCore 0:
  92.0 39.7 all-gather.2
  163.7 22.2 all-gather.4
  294.0 78.5 reduce-scatter.2
  374.7 110.5 reduce-scatter.4
  488.7 69.3 all-reduce.10

commit v2 on v1

--- a/solution.py
+++ b/solution.py
@@ -21,6 +21,7 @@
 GROUP = 5
 VMEM_LIMIT = 60 * 1024 * 1024
 
+MESH = pl.DeviceIdType.MESH
 BF = jnp.bfloat16
 F32 = jnp.float32
 
@@ -319,6 +320,812 @@
     )(near_row, ev_col, ev_row, hidden, lx, dsilu, update, gs, gv, wn, vout)
 
 
+def skip_refs(kernel, first, count):
+    def wrapped(*refs):
+        return kernel(*refs[:first], *refs[first + count :])
+
+    return wrapped
+
+
+def scalar_backward_kernel(
+    shards, near_ref, lx_ref, ds_ref, gsone_ref, wn_ref, ts_ref, ns_ref, wnode_ref,
+    ratio_ref, pack_ref, rest_ref, gscal_ref, back_ref, ga_ref, gw_ref, gb_ref, pre_scr,
+):
+    nodes = gsone_ref.shape[0]
+    table = ts_ref.shape[0]
+    rows = GROUP * nodes
+
+    @pl.when(pl.program_id(0) == 0)
+    def _():
+        for ref in (ga_ref, gw_ref, gb_ref):
+            ref[...] = jnp.zeros_like(ref)
+
+    for start in range(0, D_S, 256):
+        cols = pl.ds(start, 256)
+        for first in range(0, nodes, ROW_TILE):
+            part = pl.ds(first, ROW_TILE)
+            share = gsone_ref[part, cols] * (1.0 / NEIGH)
+            acc = None
+            for k in range(GROUP):
+                g = (ds_ref[k, part, cols].astype(F32) * share).astype(BF)
+                pre_scr[pl.ds(k * nodes + first, ROW_TILE), cols] = g
+                g = g.astype(F32)
+                acc = g if acc is None else acc + g
+            gb_ref[part, cols] += acc
+    one_hot = (lax.broadcasted_iota(jnp.int32, (table, rows), 0) == near_ref[0]).astype(BF)
+    grad_pre = pre_scr[...]
+    ga_ref[...] += product(one_hot, grad_pre)
+    lx = lx_ref[...].reshape(rows, H_P)
+    gw_ref[...] += lax.dot_general(
+        lx, grad_pre, (((0,), (0,)), ((), ())), preferred_element_type=F32
+    )
+    for start, width in LANE_BLOCKS:
+        cols = pl.ds(start, width)
+        grad_length = product_back(grad_pre, wn_ref[cols, :])
+        for first in range(0, nodes, ROW_TILE):
+            part = pl.ds(first, ROW_TILE)
+            for k in range(GROUP):
+                at = k * nodes + first
+                ratio = grad_length[at : at + ROW_TILE] * pl.reciprocal(
+                    lx_ref[k, part, cols].astype(F32), approx=True
+                )
+                if start == 512:
+                    lane = lax.broadcasted_iota(jnp.int32, (ROW_TILE, width), 1)
+                    ratio = jnp.where(lane == 0, ratio, 0.0)
+                ratio_ref[k, part, cols] = ratio.astype(BF)
+
+    @pl.when(pl.program_id(0) == pl.num_programs(0) - 1)
+    def _():
+        ga = ga_ref[...].astype(BF)
+        gb = gb_ref[...].astype(BF)
+        tall = D_S // shards
+        for half, (left, right) in enumerate(((ts_ref, ga), (ns_ref, gb))):
+            for start in range(0, D_S, 512):
+                block = lax.dot_general(
+                    left[...], right[:, start : start + 512], (((0,), (0,)), ((), ())),
+                    preferred_element_type=F32,
+                ).astype(BF)
+                at = (half * (D_S // 512) + start // 512) * tall
+                for p in range(shards):
+                    pack_ref[p, pl.ds(at, tall), :] = block[p * tall : (p + 1) * tall]
+        base = 2 * (D_S // 512) * tall
+        for p in range(shards):
+            own = pl.ds(p * tall, tall)
+            for r in range(4):
+                pack_ref[p, pl.ds(base, 128), pl.ds(r * 128, 128)] = gw_ref[
+                    pl.ds(r * 128, 128), own
+                ].astype(BF)
+            rest_ref[p] = gw_ref[pl.ds(512, 64), own].astype(BF)
+        own_part = gsone_ref[...] + product_back(gb, wnode_ref[:, pl.ds(D_S, D_S)])
+        projected = product_back(ga, wnode_ref[:, pl.ds(0, D_S)])
+        gscal_ref[...] = own_part + projected[:nodes]
+        back_ref[...] = projected[nodes:].astype(BF)
+
+
+def scalar_backward(shards, near_row, lx, dsilu, gsone, wn, table_s, node_scalar, w_node, *before):
+    nodes = gsone.shape[0]
+    table = table_s.shape[0]
+    rows = GROUP * nodes
+    whole = lambda shape: pl.BlockSpec(shape, lambda g: (0,) * len(shape))
+    slots = lambda *shape: pl.BlockSpec((GROUP,) + shape, lambda g: (g,) + (0,) * len(shape))
+    steps = lambda *shape: pl.BlockSpec((1,) + shape, lambda g: (g,) + (0,) * len(shape))
+    pack_rows = 2 * (D_S // 512) * (D_S // shards) + 128
+    outs = [
+        ((shards, pack_rows, 512), BF),
+        ((shards, 64, D_S // shards), BF),
+        ((nodes, D_S), F32),
+        ((table - nodes, D_S), BF),
+    ]
+    return pl.pallas_call(
+        skip_refs(functools.partial(scalar_backward_kernel, shards), 8, len(before)),
+        grid=(NEIGH // GROUP,),
+        in_specs=[
+            steps(1, rows),
+            slots(nodes, H_P),
+            slots(nodes, D_S),
+            whole((nodes, D_S)),
+            whole((H_P, D_S)),
+            whole((table, D_S)),
+            whole((nodes, D_S)),
+            whole((D_S, 2 * D_S)),
+        ]
+        + [pl.BlockSpec(memory_space=pl.ANY)] * len(before),
+        out_specs=[slots(nodes, H_P)] + [whole(shape) for shape, kind in outs],
+        out_shape=[jax.ShapeDtypeStruct((NEIGH, nodes, H_P), BF)]
+        + [jax.ShapeDtypeStruct(shape, kind) for shape, kind in outs],
+        scratch_shapes=[
+            pltpu.VMEM((table, D_S), F32),
+            pltpu.VMEM((H_P, D_S), F32),
+            pltpu.VMEM((nodes, D_S), F32),
+            pltpu.VMEM((rows, D_S), BF),
+        ],
+        compiler_params=pltpu.CompilerParams(vmem_limit_bytes=VMEM_LIMIT),
+        cost_estimate=pl.CostEstimate(
+            flops=2 * NEIGH * nodes * D_S * (table + 2 * H_P), bytes_accessed=30 << 20,
+            transcendentals=NEIGH * nodes * H_P,
+        ),
+        name="scalar_backward",
+    )(near_row, lx, dsilu, gsone, wn, table_s, node_scalar, w_node, *before)
+
+
+def vector_backward_kernel(
+    shards, near_ref, ev_ref, evr_ref, h_ref, ratio_ref, z_ref, gvone_ref, vo_ref, tv_ref,
+    nv_ref, vs_ref, vt_ref, rest_ref, gains_ref,
+    pack_ref, gvec_ref, back_ref, gp_ref, gq_ref, gvo_ref, up_scr, gh_scr,
+):
+    nodes = gvone_ref.shape[1]
+    table = tv_ref.shape[1]
+    rows = GROUP * nodes
+
+    @pl.when(pl.program_id(0) == 0)
+    def _():
+        for ref in (gp_ref, gq_ref, gvo_ref):
+            ref[...] = jnp.zeros_like(ref)
+
+    for first in range(0, nodes, ROW_TILE):
+        part = pl.ds(first, ROW_TILE)
+        share = [gvone_ref[c, part, :] * (1.0 / NEIGH) for c in range(3)]
+        for k in range(GROUP):
+            z = [z_ref[k, c, part, :].astype(F32) for c in range(3)]
+            power = z[0] * z[0] + z[1] * z[1] + z[2] * z[2] + 1.0
+            inverse = lax.rsqrt(power)
+            s = sigmoid(power * inverse)
+            dot = z[0] * share[0] + z[1] * share[1] + z[2] * share[2]
+            factor = dot * inverse * (s * (1.0 - s))
+            for c in range(3):
+                up_scr[c, pl.ds(k * nodes + first, ROW_TILE), :] = (
+                    share[c] * s + z[c] * factor
+                ).astype(BF)
+    for start, width in LANE_BLOCKS:
+        cols = pl.ds(start, width)
+        grad_direct = [product_back(up_scr[c], vo_ref[cols, :]) for c in range(3)]
+        for first in range(0, nodes, ROW_TILE):
+            part = pl.ds(first, ROW_TILE)
+            acc = [None] * 3
+            for k in range(GROUP):
+                at = k * nodes + first
+                ratio = ratio_ref[k, part, cols].astype(F32)
+                for c in range(3):
+                    g = grad_direct[c][at : at + ROW_TILE] + ratio * h_ref[
+                        k, c, part, cols
+                    ].astype(F32)
+                    gh_scr[c, pl.ds(at, ROW_TILE), cols] = g.astype(BF)
+                    acc[c] = g if acc[c] is None else acc[c] + g
+            for c in range(3):
+                gq_ref[c, part, cols] += acc[c]
+    one_hot = (lax.broadcasted_iota(jnp.int32, (table, rows), 0) == near_ref[0]).astype(BF)
+    for c in range(3):
+        evr = jnp.broadcast_to(evr_ref[0, c : c + 1, :], (16, rows))
+        lead = jnp.concatenate([one_hot, evr.astype(BF)], axis=0)
+        gp_ref[c] += product(lead, gh_scr[c])
+        gvo_ref[...] += lax.dot_general(
+            up_scr[c],
+            h_ref[:, c, :, :].reshape(rows, H_P),
+            (((0,), (0,)), ((), ())),
+            preferred_element_type=F32,
+        )
+
+    @pl.when(pl.program_id(0) == pl.num_programs(0) - 1)
+    def _():
+        tall = D_V // shards
+        grads = []
+        gp = [gp_ref[c, pl.ds(0, table), :].astype(BF) for c in range(3)]
+        gq = [gq_ref[c].astype(BF) for c in range(3)]
+        for lead_ref, right in ((tv_ref, gp), (nv_ref, gq)):
+            total = None
+            for c in range(3):
+                one = lax.dot_general(
+                    lead_ref[c], right[c], (((0,), (0,)), ((), ())), preferred_element_type=F32
+                )
+                total = one if total is None else total + one
+            grads.append(total)
+        grads.append(gvo_ref[...])
+        lane = lax.broadcasted_iota(jnp.int32, (D_V, 128), 1)
+        tails = jnp.zeros((D_V, 128), F32)
+        for n, grad in enumerate(grads):
+            for p in range(shards):
+                pack_ref[p, pl.ds(n * tall, tall), :] = grad[
+                    p * tall : (p + 1) * tall, :512
+                ].astype(BF)
+            tails = tails + jnp.where(
+                lane == n, jnp.broadcast_to(grad[:, 512:513], (D_V, 128)), 0.0
+            )
+        tails = tails.astype(BF)
+        vedge = gp_ref[0, pl.ds(table, 8), :] + gp_ref[1, pl.ds(table, 8), :]
+        vedge = vedge + gp_ref[2, pl.ds(table, 8), :]
+        row = lax.broadcasted_iota(jnp.int32, (tall, 128), 0)
+        for p in range(shards):
+            at = pl.ds(3 * tall, tall)
+            rest = rest_ref[p].astype(F32)
+            pack_ref[p, at, pl.ds(0, 128)] = tails[p * tall : (p + 1) * tall]
+            pack_ref[p, at, pl.ds(128, 128)] = rest[1 : 1 + tall].astype(BF)
+            extra = jnp.where(row == 0, jnp.broadcast_to(rest[0:1], (tall, 128)), 0.0)
+            for n in range(5):
+                piece = jnp.broadcast_to(vedge[0:1, n * 128 : (n + 1) * 128], (tall, 128))
+                extra = jnp.where(row == 1 + n, piece, extra)
+            for n in range(2):
+                piece = jnp.broadcast_to(gains_ref[n : n + 1, p * 128 : (p + 1) * 128], (tall, 128))
+                extra = jnp.where(row == 6 + n, piece, extra)
+            pack_ref[p, at, pl.ds(256, 128)] = extra.astype(BF)
+            pack_ref[p, at, pl.ds(384, 128)] = jnp.zeros((tall, 128), BF)
+        for c in range(3):
+            projected = product_back(gp[c], vs_ref[...])
+            gvec_ref[c] = (
+                gvone_ref[c] + product_back(gq[c], vt_ref[...]) + projected[:nodes]
+            )
+            back_ref[:, pl.ds(c * D_V, D_V)] = projected[nodes:].astype(BF)
+
+
+def vector_backward(
+    shards, near_row, ev_col, ev_row, hidden, ratio, update, gvone, vout, table_v, node_vector,
+    vec_source, vec_target, rest, gains, *before,
+):
+    nodes = gvone.shape[1]
+    table = table_v.shape[1]
+    rows = GROUP * nodes
+    whole = lambda shape: pl.BlockSpec(shape, lambda g: (0,) * len(shape))
+    slots = lambda *shape: pl.BlockSpec((GROUP,) + shape, lambda g: (g,) + (0,) * len(shape))
+    steps = lambda *shape: pl.BlockSpec((1,) + shape, lambda g: (g,) + (0,) * len(shape))
+    outs = [
+        ((shards, 4 * (D_V // shards), 512), BF),
+        ((3, nodes, D_V), F32),
+        ((table - nodes, 3 * D_V), BF),
+    ]
+    return pl.pallas_call(
+        skip_refs(functools.partial(vector_backward_kernel, shards), 14, len(before)),
+        grid=(NEIGH // GROUP,),
+        in_specs=[
+            steps(1, rows),
+            slots(nodes, 3),
+            steps(3, rows),
+            slots(3, nodes, H_P),
+            slots(nodes, H_P),
+            slots(3, nodes, D_V),
+            whole((3, nodes, D_V)),
+            whole((H_P, D_V)),
+            whole((3, table, D_V)),
+            whole((3, nodes, D_V)),
+            whole((D_V, H_P)),
+            whole((D_V, H_P)),
+            whole((shards, 64, D_S // shards)),
+            whole((8, D_S)),
+        ]
+        + [pl.BlockSpec(memory_space=pl.ANY)] * len(before),
+        out_specs=[whole(shape) for shape, kind in outs],
+        out_shape=[jax.ShapeDtypeStruct(shape, kind) for shape, kind in outs],
+        scratch_shapes=[
+            pltpu.VMEM((3, table + 16, H_P), F32),
+            pltpu.VMEM((3, nodes, H_P), F32),
+            pltpu.VMEM((D_V, H_P), F32),
+            pltpu.VMEM((3, rows, D_V), BF),
+            pltpu.VMEM((3, rows, H_P), BF),
+        ],
+        compiler_params=pltpu.CompilerParams(vmem_limit_bytes=VMEM_LIMIT),
+        cost_estimate=pl.CostEstimate(
+            flops=2 * NEIGH * nodes * 3 * H_P * (table + 2 * D_V), bytes_accessed=30 << 20,
+            transcendentals=NEIGH * nodes * D_V,
+        ),
+        name="vector_backward",
+    )(
+        near_row, ev_col, ev_row, hidden, ratio, update, gvone, vout, table_v, node_vector,
+        vec_source, vec_target, rest, gains, *before,
+    )
+
+
+def flip(count, bit):
+    return [(i, i ^ bit) for i in range(count)]
+
+
+def own_index():
+    space = lax.axis_index("space")
+    dp = lax.axis_index("dp")
+    return {"core": space % 2, "z_lo": space // 2 % 2, "z_hi": space // 4, "x": dp % 2, "y": dp // 2}
+
+
+STEP_OF = {
+    "core": ("space", 8, 1), "z_lo": ("space", 8, 2), "z_hi": ("space", 8, 4),
+    "x": ("dp", 4, 1), "y": ("dp", 4, 2),
+}
+
+
+def swap(values, way):
+    axis, count, bit = STEP_OF[way]
+    return lax.ppermute(values, axis, flip(count, bit))
+
+
+def halve(values, way, dim):
+    mine = own_index()[way]
+    away = lax.dynamic_index_in_dim(values, 1 - mine, dim, False)
+    kept = lax.dynamic_index_in_dim(values, mine, dim, False)
+    return (kept.astype(F32) + swap(away, way).astype(F32)).astype(BF)
+
+
+def reduce_core(packed):
+    shards, rows, width = packed.shape
+    return halve(packed.reshape(shards // 2, 2, rows, width), "core", 1)
+
+
+def reduce_first(values):
+    quads, rows, width = values.shape
+    parts = values.reshape(quads, 2, 2, rows // 4, width)
+    return halve(parts[:, 0], "x", 1), halve(parts[:, 1], "y", 1)
+
+
+def reduce_second(pair):
+    quads, rows, width = pair[0].shape
+    shape = (quads, 2, rows // 2, width)
+    return halve(pair[0].reshape(shape), "y", 1), halve(pair[1].reshape(shape), "x", 1)
+
+
+def reduce_z(values):
+    quads, rows, width = values.shape
+    values = halve(values.reshape(2, 2, rows, width), "z_lo", 1)
+    return halve(values, "z_hi", 0)
+
+
+def join(values, way, axis=0):
+    other = swap(values, way)
+    mine = own_index()[way]
+    return jnp.stack([jnp.where(mine == 0, values, other), jnp.where(mine == 0, other, values)], axis)
+
+
+def gather_plane(first, second):
+    first = join(join(first, "y"), "x")
+    second = join(join(second, "x"), "y")
+    return jnp.concatenate([first.reshape(-1, 512), second.reshape(-1, 512)], 0)
+
+
+def full_block(shape):
+    return pl.BlockSpec(shape, lambda: (0,) * len(shape))
+
+
+def lead_product(former, latter):
+    return lax.dot_general(
+        former, latter, (((0,), (0,)), ((), ())), preferred_element_type=F32
+    )
+
+
+def swap_halves(values):
+    return pltpu.roll(values, 64, 1)
+
+
+def lower_half(shape):
+    return lax.broadcasted_iota(jnp.int32, shape, 1) < 64
+
+
+def pack_tall(tile, odd):
+    rows = tile.shape[0] // 2
+    top, low = tile[:rows], tile[rows:]
+    side = lower_half((rows, 128))
+    if odd:
+        return jnp.where(side, swap_halves(top), low)
+    return jnp.where(side, top, swap_halves(low))
+
+
+def unpack_tall(block):
+    rows = block.shape[0]
+    side = lower_half((rows, 128))
+    return jnp.concatenate(
+        [jnp.where(side, block, 0.0), jnp.where(side, swap_halves(block), 0.0)], 0
+    )
+
+
+def centre(values):
+    centred = values - jnp.mean(values, axis=-1, keepdims=True)
+    inverse = lax.rsqrt(jnp.mean(centred * centred, axis=-1, keepdims=True) + 1e-05)
+    return centred * inverse, inverse
+
+
+def centre_back(hat, inverse, grad):
+    return inverse * (
+        grad
+        - jnp.mean(grad, axis=-1, keepdims=True)
+        - hat * jnp.mean(grad * hat, axis=-1, keepdims=True)
+    )
+
+
+def power_of(parts):
+    return parts[0] * parts[0] + parts[1] * parts[1] + parts[2] * parts[2]
+
+
+def node_forward_kernel(
+    ns_ref, nv_ref, as_ref, av_ref, ng_ref, fv_ref, fs_ref, fu_ref, we_ref, ag_ref, wq_ref,
+    s1_ref, v1_ref, ffin_ref, ffh_ref, ffp_ref, ffu_ref, v2_ref, emb_ref, sz_ref, ain_ref, out_ref,
+):
+    nodes = ns_ref.shape[0]
+    s1 = ns_ref[...].astype(F32) + as_ref[...]
+    s1_ref[...] = s1
+    hat, unused = centre(s1)
+    normed_s = hat * ng_ref[...]
+    v1 = [nv_ref[c].astype(F32) + av_ref[c] for c in range(3)]
+    scale = lax.rsqrt(jnp.mean(power_of(v1), axis=-1, keepdims=True) + 1e-05)
+    normed_v = [v * scale for v in v1]
+    ffh = [product(v.astype(BF), fv_ref[...]) for v in normed_v]
+    power = power_of(ffh) + 1.0
+    ffin_ref[:, pl.ds(0, D_S)] = normed_s.astype(BF)
+    ffin_ref[:, pl.ds(D_S, D_V)] = (power * lax.rsqrt(power)).astype(BF)
+    ffp = product(ffin_ref[...], fs_ref[...])
+    ffu = [product(h.astype(BF), fu_ref[...]) for h in ffh]
+    for c in range(3):
+        v1_ref[c] = v1[c]
+        ffh_ref[c] = ffh[c]
+        ffu_ref[c] = ffu[c]
+    ffp_ref[...] = ffp
+    s2 = normed_s + ffp * sigmoid(ffp)
+    power = power_of(ffu) + 1.0
+    gate = sigmoid(power * lax.rsqrt(power))
+    v2 = [normed_v[c] + ffu[c] * gate for c in range(3)]
+    for c in range(3):
+        v2_ref[c] = v2[c]
+    power = power_of(v2) + 1.0
+    emb_ref[:, pl.ds(0, D_S)] = s2.astype(BF)
+    emb_ref[:, pl.ds(D_S, D_V)] = (power * lax.rsqrt(power)).astype(BF)
+    sz = product(emb_ref[...], we_ref[...])
+    sz_ref[...] = sz
+    hat, unused = centre(sz)
+    attn_in = (hat * ag_ref[...]).astype(BF)
+    ain_ref[...] = attn_in
+    q, k, v = [product(attn_in, wq_ref[:, pl.ds(n * D_MODEL, D_MODEL)]) for n in range(3)]
+    pack_heads(q, k, v, out_ref)
+
+
+def pack_heads(q, k, v, out_ref):
+    nodes = q.shape[0]
+    side = lower_half((nodes, 128))
+    for pair in range(HEADS // 2):
+        cols = slice(pair * 128, pair * 128 + 128)
+        qp, kp, vp = q[:, cols], k[:, cols], v[:, cols]
+        even = jnp.where(side, qp, swap_halves(kp))
+        odd = jnp.where(side, swap_halves(qp), kp)
+        for n, block in enumerate((even, odd)):
+            head = 2 * pair + n
+            out_ref[head, pl.ds(0, nodes), :] = block.astype(BF)
+            out_ref[head, pl.ds(nodes, nodes // 2), :] = pack_tall(vp, n == 1).astype(BF)
+
+
+def node_forward(node_scalar, node_vector, agg_s, agg_v, *weights):
+    nodes = node_scalar.shape[0]
+    outs = [
+        ((nodes, D_S), F32),
+        ((3, nodes, D_V), F32),
+        ((nodes, D_S + D_V), BF),
+        ((3, nodes, D_V), F32),
+        ((nodes, D_S), F32),
+        ((3, nodes, D_V), F32),
+        ((3, nodes, D_V), F32),
+        ((nodes, D_S + D_V), BF),
+        ((nodes, D_MODEL), F32),
+        ((nodes, D_MODEL), BF),
+        ((HEADS, nodes + nodes // 2, 128), BF),
+    ]
+    return pl.pallas_call(
+        node_forward_kernel,
+        out_shape=[jax.ShapeDtypeStruct(shape, kind) for shape, kind in outs],
+        compiler_params=pltpu.CompilerParams(vmem_limit_bytes=VMEM_LIMIT),
+        name="node_forward",
+    )(node_scalar, node_vector, agg_s, agg_v, *weights)
+
+
+def exchange_kernel(spaces, x_ref, y_ref, send_sem, recv_sem, own_sem):
+    me = lax.axis_index("space")
+    barrier = pltpu.get_barrier_semaphore()
+    peers = [lax.rem(me + d, spaces) for d in range(1, spaces)]
+    for peer in peers:
+        pl.semaphore_signal(barrier, inc=1, device_id={"space": peer}, device_id_type=MESH)
+    own = pltpu.make_async_copy(x_ref.at[me], y_ref.at[me], own_sem)
+    own.start()
+    pl.semaphore_wait(barrier, spaces - 1)
+    copies = []
+    for n, peer in enumerate(peers):
+        copies.append(
+            pltpu.make_async_remote_copy(
+                src_ref=x_ref.at[peer],
+                dst_ref=y_ref.at[me],
+                send_sem=send_sem.at[n],
+                recv_sem=recv_sem.at[n],
+                device_id={"space": peer},
+                device_id_type=MESH,
+            )
+        )
+        copies[-1].start()
+    own.wait()
+    for copy in copies:
+        copy.wait()
+
+
+def exchange(values, collective_id):
+    spaces = values.shape[0]
+    return pl.pallas_call(
+        functools.partial(exchange_kernel, spaces),
+        out_shape=jax.ShapeDtypeStruct(values.shape, values.dtype),
+        in_specs=[pl.BlockSpec(memory_space=pl.ANY)],
+        out_specs=pl.BlockSpec(memory_space=pl.ANY),
+        scratch_shapes=[
+            pltpu.SemaphoreType.DMA((spaces - 1,)),
+            pltpu.SemaphoreType.DMA((spaces - 1,)),
+            pltpu.SemaphoreType.DMA,
+        ],
+        compiler_params=pltpu.CompilerParams(collective_id=collective_id, has_side_effects=True),
+        name="exchange",
+    )(values)
+
+
+def split_heads(x_ref, nodes):
+    spaces = x_ref.shape[0]
+    both = x_ref[:, pl.ds(0, nodes), :].reshape(spaces * nodes, 128).astype(F32)
+    queries = jnp.where(lower_half(both.shape), both, 0.0).astype(BF)
+    keys = swap_halves(both).astype(BF)
+    values = jnp.concatenate(
+        [unpack_tall(x_ref[d, pl.ds(nodes, nodes // 2), :].astype(F32)) for d in range(spaces)], 0
+    ).astype(BF)
+    return queries, keys, values
+
+
+def attend_kernel(x_ref, id_ref, probs_ref, att_ref, out_ref):
+    spaces = x_ref.shape[0]
+    nodes = x_ref.shape[1] * 2 // 3
+    count = spaces * nodes
+    queries, keys, values = split_heads(x_ref, nodes)
+    row_ids = id_ref[...]
+    column_ids = jnp.transpose(jnp.broadcast_to(row_ids, (8, count)))[:, 0:1]
+    block = 2 * nodes
+    for first in range(0, count, block):
+        scores = product_back(queries[first : first + block], keys) * HEAD_DIM ** (-0.5)
+        same = column_ids[first : first + block] == row_ids
+        scores = jnp.where(same, scores, -1000000000.0)
+        shifted = jnp.exp(scores - jnp.max(scores, axis=-1, keepdims=True))
+        probs = (shifted / jnp.sum(shifted, axis=-1, keepdims=True)).astype(BF)
+        probs_ref[pl.ds(first, block), :] = probs
+        att = product(probs, values)
+        att_ref[pl.ds(first, block), :] = att
+        for n in range(block // nodes):
+            tile = att[n * nodes : (n + 1) * nodes]
+            out_ref[first // nodes + n] = pack_tall(tile, False).astype(BF)
+
+
+def attend(heads_in, ids):
+    spaces, tall, unused = heads_in.shape
+    nodes = tall * 2 // 3
+    count = spaces * nodes
+    outs = [((count, count), BF), ((count, 128), F32), ((spaces, nodes // 2, 128), BF)]
+    return pl.pallas_call(
+        attend_kernel,
+        out_shape=[jax.ShapeDtypeStruct(shape, kind) for shape, kind in outs],
+        compiler_params=pltpu.CompilerParams(vmem_limit_bytes=VMEM_LIMIT),
+        name="attend",
+    )(heads_in, ids)
+
+
+def attend_backward_kernel(x_ref, probs_ref, att_ref, g_ref, out_ref, gs_scr):
+    spaces = x_ref.shape[0]
+    nodes = x_ref.shape[1] * 2 // 3
+    count = spaces * nodes
+    queries, keys, values = split_heads(x_ref, nodes)
+    grad = jnp.concatenate(
+        [unpack_tall(g_ref[d].astype(F32)) for d in range(spaces)], 0
+    )
+    dots = jnp.sum(grad * att_ref[...], axis=-1, keepdims=True)
+    grad = grad.astype(BF)
+    block = 2 * nodes
+    scale = HEAD_DIM ** (-0.5)
+    grad_queries = []
+    for first in range(0, count, block):
+        grad_probs = product_back(grad[first : first + block], values)
+        part = probs_ref[pl.ds(first, block), :].astype(F32)
+        grad_scores = (part * (grad_probs - dots[first : first + block])).astype(BF)
+        gs_scr[pl.ds(first, block), :] = grad_scores
+        grad_queries.append(product(grad_scores, keys))
+    grad_queries = jnp.concatenate(grad_queries, 0) * scale
+    grad_keys = jnp.transpose(lead_product(queries, gs_scr[...])) * scale
+    grad_values = jnp.transpose(lead_product(grad, probs_ref[...]))
+    side = lower_half((nodes, 128))
+    for d in range(spaces):
+        rows = slice(d * nodes, (d + 1) * nodes)
+        out_ref[d, pl.ds(0, nodes), :] = jnp.where(
+            side, grad_queries[rows], swap_halves(grad_keys[rows])
+        ).astype(BF)
+        out_ref[d, pl.ds(nodes, nodes // 2), :] = pack_tall(grad_values[rows], False).astype(BF)
+
+
+def attend_backward(heads_in, probs, att, grad_in, *before):
+    count = probs.shape[0]
+    return pl.pallas_call(
+        skip_refs(attend_backward_kernel, 4, len(before)),
+        in_specs=[pl.BlockSpec(memory_space=pltpu.VMEM)] * 4
+        + [pl.BlockSpec(memory_space=pl.ANY)] * len(before),
+        out_shape=jax.ShapeDtypeStruct(heads_in.shape, BF),
+        scratch_shapes=[pltpu.VMEM((count, count), BF)],
+        compiler_params=pltpu.CompilerParams(vmem_limit_bytes=VMEM_LIMIT),
+        name="attend_backward",
+    )(heads_in, probs, att, grad_in, *before)
+
+
+def merge_heads(block_ref, first, half):
+    tiles = []
+    for pair in range(HEADS // 2):
+        even = unpack_tall(block_ref[2 * pair, pl.ds(first, half), :].astype(F32))
+        odd = unpack_tall(block_ref[2 * pair + 1, pl.ds(first, half), :].astype(F32))
+        tiles.append(even + swap_halves(odd))
+    return jnp.concatenate(tiles, 1)
+
+
+def feed_kernel(
+    att_ref, sz_ref, wo_ref, fg_ref, wu_ref, wd_ref, cot_ref,
+    out_ref, pack_ref, gatt_ref, gs1_ref, attr_ref, gbr_ref, ggain_ref, gelu_scr, gup_scr,
+):
+    nodes = sz_ref.shape[0]
+    shards = pack_ref.shape[0]
+    att = merge_heads(att_ref, 0, nodes // 2).astype(BF)
+    attr_ref[...] = att
+    stream_one = sz_ref[...] + product(att, wo_ref[...])
+    hat, inverse = centre(stream_one)
+    ffn_in = (hat * fg_ref[...]).astype(BF)
+    ffn = wu_ref.shape[1]
+    cot = cot_ref[...]
+    for start in range(0, ffn, 512):
+        cols = pl.ds(start, 512)
+        x = product(ffn_in, wu_ref[:, cols])
+        cdf = 0.5 * (1.0 + lax.erf(x * (0.5**0.5)))
+        gelu_scr[:, cols] = (x * cdf).astype(BF)
+        slope = cdf + x * jnp.exp(-0.5 * x * x) * ((0.5 / math.pi) ** 0.5)
+        gup_scr[:, cols] = (product_back(cot, wd_ref[cols, :]) * slope).astype(BF)
+    out_ref[...] = (stream_one + product(gelu_scr[...], wd_ref[...])).astype(BF)
+    grad_in = product_back(gup_scr[...], wu_ref[...])
+    ggain_ref[...] = jnp.sum(grad_in * hat, axis=0, keepdims=True)
+    grad_one = cot.astype(F32) + centre_back(hat, inverse, grad_in * fg_ref[...])
+    gs1_ref[...] = grad_one
+    branch = grad_one.astype(BF)
+    gbr_ref[...] = branch
+    grad_att = product_back(branch, wo_ref[...])
+    for head in range(HEADS):
+        tile = grad_att[:, head // 2 * 128 : head // 2 * 128 + 128]
+        gatt_ref[head] = pack_tall(tile, head % 2 == 1).astype(BF)
+    tall = ffn // shards
+    for start in range(0, ffn, 512):
+        block = lead_product(gelu_scr[:, pl.ds(start, 512)], cot).astype(BF)
+        for n in range(512 // tall):
+            pack_ref[start // tall + n, pl.ds(0, tall), :] = block[n * tall : (n + 1) * tall]
+        block = lead_product(ffn_in, gup_scr[:, pl.ds(start, 512)]).astype(BF)
+        low = D_MODEL // shards
+        for p in range(shards):
+            pack_ref[p, pl.ds(tall + start // 512 * low, low), :] = block[p * low : (p + 1) * low]
+
+
+def feed(att_in, stream_zero, w_out, gain, w_up, w_down, cotangent):
+    nodes = stream_zero.shape[0]
+    shards = att_in.shape[0]
+    ffn = w_up.shape[1]
+    tall = ffn // shards + (ffn // 512) * (D_MODEL // shards)
+    outs = [
+        ((nodes, D_MODEL), BF),
+        ((shards, tall, 512), BF),
+        (att_in.shape, BF),
+        ((nodes, D_MODEL), F32),
+        ((nodes, D_MODEL), BF),
+        ((nodes, D_MODEL), BF),
+        ((1, D_MODEL), F32),
+    ]
+    return pl.pallas_call(
+        feed_kernel,
+        out_shape=[jax.ShapeDtypeStruct(shape, kind) for shape, kind in outs],
+        scratch_shapes=[pltpu.VMEM((nodes, ffn), BF), pltpu.VMEM((nodes, ffn), BF)],
+        compiler_params=pltpu.CompilerParams(vmem_limit_bytes=VMEM_LIMIT),
+        name="feed",
+    )(att_in, stream_zero, w_out, gain, w_up, w_down, cotangent)
+
+
+def node_backward_kernel(
+    gq_ref, gs1_ref, attr_ref, gbr_ref, s1_ref, v1_ref, ffin_ref, ffh_ref, ffp_ref, ffu_ref, v2_ref,
+    emb_ref, sz_ref, ain_ref, ng_ref, fv_ref, fs_ref, fu_ref, we_ref, ag_ref, wq_ref, fgain_ref,
+    pack_ref, gsone_ref, gvone_ref, gains_ref,
+):
+    nodes = gs1_ref.shape[0]
+    shards = pack_ref.shape[0]
+    side = lower_half((nodes, 128))
+    tiles = [[], []]
+    for pair in range(HEADS // 2):
+        even = gq_ref[2 * pair, pl.ds(0, nodes), :].astype(F32)
+        odd = gq_ref[2 * pair + 1, pl.ds(0, nodes), :].astype(F32)
+        tiles[0].append(jnp.where(side, even, swap_halves(odd)))
+        tiles[1].append(jnp.where(side, swap_halves(even), odd))
+    grads = [jnp.concatenate(tile, 1).astype(BF) for tile in tiles]
+    grads.append(merge_heads(gq_ref, nodes, nodes // 2).astype(BF))
+    attn_in = ain_ref[...]
+    grad_in = None
+    low = D_MODEL // shards
+    base = 0
+
+    def put(grad, height):
+        nonlocal base
+        grad = grad.astype(BF)
+        for p in range(shards):
+            pack_ref[p, pl.ds(base, height), :] = grad[p * height : (p + 1) * height]
+        base += height
+
+    for n in range(3):
+        one = product_back(grads[n], wq_ref[:, pl.ds(n * D_MODEL, D_MODEL)])
+        grad_in = one if grad_in is None else grad_in + one
+        put(lead_product(attn_in, grads[n]), low)
+    put(lead_product(attr_ref[...], gbr_ref[...]), low)
+    hat, inverse = centre(sz_ref[...])
+    grad_attn_gain = jnp.sum(grad_in * hat, axis=0, keepdims=True)
+    stream = gs1_ref[...] + centre_back(hat, inverse, grad_in * ag_ref[...])
+    stream = stream.astype(BF)
+    put(lead_product(emb_ref[...], stream), (D_S + D_V) // shards)
+    grad_emb = product_back(stream, we_ref[...])
+    grad_s2, grad_len = grad_emb[:, :D_S], grad_emb[:, D_S:]
+    v2 = [v2_ref[c] for c in range(3)]
+    factor = grad_len * lax.rsqrt(power_of(v2) + 1.0)
+    grad_v2 = [factor * v for v in v2]
+    x = ffp_ref[...]
+    s = sigmoid(x)
+    grad_pre = (grad_s2 * (s + x * s * (1.0 - s))).astype(BF)
+    for start in range(0, D_S, 512):
+        put(lead_product(ffin_ref[...], grad_pre[:, start : start + 512]), (D_S + D_V) // shards)
+    grad_ffin = product_back(grad_pre, fs_ref[...])
+    z = [ffu_ref[c] for c in range(3)]
+    power = power_of(z) + 1.0
+    inverse = lax.rsqrt(power)
+    s = sigmoid(power * inverse)
+    dot = z[0] * grad_v2[0] + z[1] * grad_v2[1] + z[2] * grad_v2[2]
+    factor = dot * inverse * (s * (1.0 - s))
+    grad_up = [(grad_v2[c] * s + z[c] * factor).astype(BF) for c in range(3)]
+    h = [ffh_ref[c] for c in range(3)]
+    factor = grad_ffin[:, D_S:] * lax.rsqrt(power_of(h) + 1.0)
+    v1 = [v1_ref[c] for c in range(3)]
+    scale = lax.rsqrt(jnp.mean(power_of(v1), axis=-1, keepdims=True) + 1e-05)
+    up_total = vec_total = None
+    grad_nv = []
+    for c in range(3):
+        one = lead_product(h[c].astype(BF), grad_up[c])
+        up_total = one if up_total is None else up_total + one
+        grad_h = (product_back(grad_up[c], fu_ref[...]) + factor * h[c]).astype(BF)
+        one = lead_product((v1[c] * scale).astype(BF), grad_h)
+        vec_total = one if vec_total is None else vec_total + one
+        grad_nv.append(grad_v2[c] + product_back(grad_h, fv_ref[...]))
+    put(jnp.concatenate([vec_total, up_total], 1), D_V // shards)
+    grad_ns = grad_s2 + grad_ffin[:, :D_S]
+    hat, inverse = centre(s1_ref[...])
+    grad_norm_gain = jnp.sum(grad_ns * hat, axis=0, keepdims=True)
+    gsone_ref[...] = centre_back(hat, inverse, grad_ns * ng_ref[...])
+    dot = grad_nv[0] * v1[0] + grad_nv[1] * v1[1] + grad_nv[2] * v1[2]
+    dot = jnp.mean(dot, axis=-1, keepdims=True) * scale * scale
+    for c in range(3):
+        gvone_ref[c] = scale * (grad_nv[c] - v1[c] * dot)
+    gains_ref[...] = jnp.zeros_like(gains_ref)
+    gains_ref[0:1, :] = grad_norm_gain
+    for p in range(shards):
+        pair = slice(p // 2 * 128, p // 2 * 128 + 128)
+        left = jnp.broadcast_to(grad_attn_gain[:, pair], (8, 128))
+        right = jnp.broadcast_to(fgain_ref[:, pair], (8, 128))
+        if p % 2 == 0:
+            both = jnp.where(lower_half((8, 128)), left, swap_halves(right))
+        else:
+            both = jnp.where(lower_half((8, 128)), swap_halves(left), right)
+        gains_ref[1:2, pl.ds(p * 128, 128)] = both[0:1]
+
+
+def node_backward(grad_heads, *values, before=()):
+    nodes = values[0].shape[0]
+    shards = grad_heads.shape[0]
+    tall = 4 * (D_MODEL // shards) + 3 * ((D_S + D_V) // shards) + D_V // shards
+    outs = [
+        ((shards, tall, 512), BF),
+        ((nodes, D_S), F32),
+        ((3, nodes, D_V), F32),
+        ((8, D_S), F32),
+    ]
+    seen = 1 + len(values)
+    return pl.pallas_call(
+        skip_refs(node_backward_kernel, seen, len(before)),
+        in_specs=[pl.BlockSpec(memory_space=pltpu.VMEM)] * seen
+        + [pl.BlockSpec(memory_space=pl.ANY)] * len(before),
+        out_shape=[jax.ShapeDtypeStruct(shape, kind) for shape, kind in outs],
+        compiler_params=pltpu.CompilerParams(vmem_limit_bytes=VMEM_LIMIT),
+        name="node_backward",
+    )(grad_heads, *values, *before)
+
+
 def pad_to(values, size, axis):
     pads = [(0, 0)] * values.ndim
     pads[axis] = (0, size - values.shape[axis])
@@ -336,6 +1143,11 @@
 def unfold(rows_in, rows, columns, width=512):
     parts = columns // width
     return jnp.moveaxis(rows_in.reshape(parts, rows, width), 0, 1).reshape(rows, columns)
+
+
+def unfold_lanes(rows_in):
+    rows, width = rows_in.shape
+    return jnp.moveaxis(rows_in.reshape(rows, width // 128, 128), 1, 0).reshape(-1, 128)
 
 
 def body(
@@ -391,6 +1203,127 @@
     agg_s, agg_v, hidden, lx, dsilu, update = edge_forward(
         near_col, es_pad, ev_col, mix, b_target, p_source, q_target, ve_row, vout
     )
+
+    if spaces == HEADS and lax.axis_size("dp") == 4 and local_rows == 128:
+        row_of = lambda gain: gain.astype(F32)[None]
+        s1, v1, ffin, ffh, ffp, ffu, v2, emb, sz, ain, heads_out = node_forward(
+            node_scalar, node_vector, agg_s, agg_v, row_of(norm_gain), ff_vec, ff_scalar, ff_up,
+            w_embed, row_of(attn_gain), w_qkv,
+        )
+        heads_in = exchange(heads_out, 0)
+        probs, att, att_out = attend(heads_in, complex_id[None])
+        stream_out, first_share, gatt, gs1, attr, gbr, fgain = feed(
+            exchange(att_out, 1), sz, w_out, row_of(ffn_gain), w_up, w_down, cotangent
+        )
+        first = reduce_core(first_share)
+        gatt_in = exchange(gatt, 1)
+        grad_heads = exchange(attend_backward(heads_in, probs, att, gatt_in, first), 0)
+        first = reduce_first(first)
+        middle_share, gsone, gvone, gains = node_backward(
+            grad_heads, gs1, attr, gbr, s1, v1, ffin, ffh, ffp, ffu, v2, emb, sz, ain,
+            row_of(norm_gain), ff_vec, ff_scalar, ff_up, w_embed, row_of(attn_gain), w_qkv, fgain,
+            before=first,
+        )
+        middle = reduce_core(middle_share)
+        first = reduce_second(first)
+        ratio, second_share, rest, gscal, back_s = scalar_backward(
+            spaces, near_row, lx, dsilu, gsone, wn_mix, table_s, node_scalar, w_node,
+            middle, *first,
+        )
+        second = reduce_core(second_share)
+        middle = reduce_first(middle)
+        third_share, gvec, back_v = vector_backward(
+            spaces, near_row, ev_col, ev_row, hidden, ratio, update, gvone, vout,
+            table_v, node_vector, vec_source, vec_target, rest, gains, second, *middle,
+        )
+        second = reduce_first(second)
+        middle = reduce_second(middle)
+        third = reduce_first(reduce_core(third_share))
+        back = jnp.concatenate([back_s, back_v], 1).reshape(spaces, CAP, D_S + 3 * D_V)
+        got = exchange(back, 2)
+        got = got.reshape(extra_rows, D_S + 3 * D_V)
+        got = jnp.where(sent_live[:, None], got, 0)
+        added = lax.dot_general(pick, got, (((0,), (0,)), ((), ())), preferred_element_type=F32)
+        grad_scalar = gscal + added[:, :D_S]
+        grad_vector = gvec + jnp.moveaxis(added[:, D_S:].reshape(local_rows, 3, D_V), 1, 0)
+        late = reduce_second(tuple(jnp.concatenate(two, 1) for two in zip(second, third)))
+        shares = [first_share, middle_share, second_share, third_share]
+        eighths = [share.shape[1] // 8 for share in shares]
+        rest_of = eighths[2] + eighths[3]
+        reduced = reduce_z(jnp.concatenate(first + middle + late, 1))
+        cuts = [0]
+        for rows in (eighths[0], eighths[0], eighths[1], eighths[1], rest_of, rest_of):
+            cuts.append(cuts[-1] + rows)
+        pieces = [reduced[lo:hi] for lo, hi in zip(cuts, cuts[1:])]
+        gathered_x = join(join(jnp.concatenate(pieces[0::2], 0), "y"), "x").reshape(4, -1, 512)
+        gathered_y = join(join(jnp.concatenate(pieces[1::2], 0), "x"), "y").reshape(4, -1, 512)
+
+        def rows_of(lo, hi, start, stop, outer):
+            halves = [
+                part[:, start:stop].reshape(outer, -1, 512)[:, lo:hi].reshape(-1, 512)
+                for part in (gathered_x, gathered_y)
+            ]
+            return jnp.concatenate(halves, 0).astype(F32)
+
+        early = eighths[0] + eighths[1]
+        first_sum = rows_of(0, eighths[0], 0, eighths[0], 4)
+        middle_sum = rows_of(0, eighths[1], eighths[0], early, 4)
+        second_sum = rows_of(0, 2 * eighths[2], early, early + rest_of, 2)
+        third_sum = rows_of(2 * eighths[2], 2 * rest_of, early, early + rest_of, 2)
+
+        def taker(rows_in):
+            at = [0]
+
+            def take(rows, cols, blocks=1):
+                part = rows_in[at[0] : at[0] + rows * blocks]
+                at[0] += rows * blocks
+                return unfold(part, rows, cols) if blocks > 1 else part
+
+            return take
+
+        take = taker(first_sum)
+        out_down = take(w_down.shape[0] // spaces, 512)
+        out_up = take(D_MODEL // spaces, 2048, 4)
+        take = taker(middle_sum)
+        out_qkv = take(D_MODEL // spaces, 1536, 3)
+        out_out = take(D_MODEL // spaces, 512)
+        out_embed = take((D_S + D_V) // spaces, 512)
+        out_ffs = take((D_S + D_V) // spaces, 1024, 2)
+        both = take(D_V // spaces, 512)
+        out_ffv, out_ffu = both[:, :D_V], both[:, D_V:]
+        take = taker(second_sum)
+        node_ab = take(D_S // spaces, 2048, 4)
+        norms_main = unfold_lanes(take(128, 512))
+        take = taker(third_sum)
+        vec_a = take(D_V // spaces, 512)
+        vec_b = take(D_V // spaces, 512)
+        vout_t = take(D_V // spaces, 512)
+        tails = take(D_V // spaces, 512)
+        out_vec_node = jnp.concatenate([vec_a, tails[:, 0:1], vec_b, tails[:, 1:2]], 1)
+        out_vec_out = jnp.concatenate([vout_t, tails[:, 2:3]], 1).T
+        misc = tails[:, 256:384]
+        return (
+            stream_out,
+            grad_scalar.astype(BF),
+            grad_vector.astype(BF),
+            node_ab,
+            tails[:, 128:256],
+            jnp.concatenate([norms_main, misc[0:1]], 0),
+            out_vec_node,
+            misc[1:6].reshape(1, 640)[:, :H_V],
+            out_vec_out,
+            misc[6],
+            out_ffv,
+            out_ffs,
+            out_ffu,
+            out_embed,
+            misc[7, :64],
+            out_qkv,
+            out_out,
+            misc[7, 64:],
+            out_up,
+            out_down,
+        )
 
     scalar_one = node_scalar.astype(F32) + agg_s
     vector_one = node_vector.astype(F32) + agg_v

time: 591 us -> 419 us (0.71)
  Pallas kernels: 79.9 us -> 194 us
  waiting for transfers between devices: 194 us -> 86.1 us
  local copies, waits for them, and re-layouts: 130 us -> 41.9 us
  matrix products: 78.6 us -> 10.5 us
  blocking collectives: 38.3 us -> 0 us
  starting transfers between devices: 11.6 us -> 31.1 us
  between operations: 16.2 us -> 1.94 us
  other arithmetic: 32.1 us -> 46 us
    reduce_scatter x2 -> x0, waiting for transfers between devices: 141 us -> none  [the longest x1 113 us: body(): lax.psum_scatter(first_share, 'space', scatter_dimension=0, tiled=False)]
    pallas_call x1 -> x12, Pallas kernels: 44.5 us -> 158 us  [the longest x5 65.7 us: exchange(): pl.pallas_call(functools.partial(exchange_kernel, spaces), out_shape=jax....]
    ppermute x0 -> x24, waiting for transfers between devices: none -> 86.1 us  [swap(): return lax.ppermute(values, axis, flip(count, bit))]
    dot_general x30 -> x0, matrix products: 60.1 us -> none  [the longest x12 21.4 us: product_back(): lax.dot_general(former, latter, (((former.ndim - 1,), (1,)), ((), ())), p...]
    psum x1 -> x0, blocking collectives: 38.3 us -> none  [body(): grad_vec_edge = lax.psum(grad_vedge[None, :], ('dp', 'space'))]
    all_gather x2 -> x0, waiting for transfers between devices: 32.9 us -> none  [the longest x1 32.9 us: body(): full_qkv = lax.all_gather(qkv, 'space', axis=0, tiled=True)]
    slice x21 -> x16, local copies, waits for them, and re-layouts: 28.1 us -> 0.86 us  [the longest x4 0.59 us: reduce_first(): return (halve(parts[:, 0], 'x', 1), halve(parts[:, 1], 'y', 1))]
    ppermute x0 -> x24, starting transfers between devices: none -> 24.8 us  [swap(): return lax.ppermute(values, axis, flip(count, bit))]
  transfers between devices with their start and end apart: 7 -> 25, of which waited for: 4 -> 12; matrix products, arithmetic and copies ran while one was open for 18% -> 11% of each run, Pallas kernels for 0% -> 20%
where the time goes in v2:
time: 419 us; the launch traced here: 412 us
  Pallas kernels  194 us (46%)
  waiting for transfers between devices  86.1 us (21%)
  other arithmetic  46 us (11%)
  local copies, waits for them, and re-layouts  41.9 us (10%)
  starting transfers between devices  31.1 us (7%)
  matrix products  10.5 us (3%)
    ppermute x24, waiting for transfers between devices, swap(): return lax.ppermute(values, axis, flip(count, bit))  86.1 us
    pallas_call x5, Pallas kernels, exchange(): pl.pallas_call(functools.partial(exchange_kernel, spaces), out_shape=jax....  65.7 us
    pallas_call x1, Pallas kernels, edge_forward(): pl.pallas_call(edge_forward_kernel, grid=(NEIGH // GROUP,), in_specs=[slo...  35.8 us
    pallas_call x1, Pallas kernels, vector_backward(): pl.pallas_call(skip_refs(functools.partial(vector_backward_kernel, shards...  29.8 us
    pallas_call x1, Pallas kernels, scalar_backward(): pl.pallas_call(skip_refs(functools.partial(scalar_backward_kernel, shards...  27.4 us
    ppermute x24, starting transfers between devices, swap(): return lax.ppermute(values, axis, flip(count, bit))  24.8 us
    convert_element_type x14, other arithmetic, halve(): return (kept.astype(F32) + swap(away, way).astype(F32)).astype(BF)  22.5 us
    squeeze x20, local copies, waits for them, and re-layouts, halve(): away = lax.dynamic_index_in_dim(values, 1 - mine, dim, False)  18.1 us
  transfers between devices with their start and end apart: 25, of which 12 were waited for; matrix products, arithmetic and copies ran while one was open for 11% of the time, Pallas kernels for 20%

profile of v2, /device:TPU:0, one launch (start us, length us, event | category | flops | bytes accessed | tf_op | source)
XLA Modules:
  0.0 411.6 jit_solution(1102452556609468117)
XLA Ops:
  4.6 6.3 %all-to-all-start = ((bf16[8,16,1792]{2,1,0:T(8,128)(2,1)}), bf16[8,16,1792]{2,1,0:T(8,128)(2,1)S(1)}, u32[]{:S(2)}, u32[]{:S(2)}) async-start(bf16[8,16,1792]{2,1,0:T(8,128)(2,1)} %bitcast.8), calls=%async_computation | async-start | bytes 917504 | tf_op jit(solution)/shard_map/all_to_all | solution.py:1171
  24.3 2.8 fusion.6.b_ref
  27.2 2.4 fusion.15
  32.5 35.8 %edge_forward.1 = (f32[128,1024]{1,0:T(8,128)}, f32[3,128,256]{2,1,0:T(8,128)}, bf16[30,3,128,640]{3,2,1,0:T(8,128)(2,1)}, bf16[30,128,640]{2,1,0:T(8,128)(2,1)}...) custom-call(s32[30,128,1]{2,1,0:T(8,128)} %copy.120.near_ref, bf16[30,128,128]{2,1,0:T(8,128)(2,1)} %pad.25.es_ref, ...), custom_call_target="tpu_custom_call" | custom-call | tf_op jit(solution)/shard_map/edge_forward/pallas_call | solution.py:162
  68.3 5.6 %node_forward.1 = (f32[128,1024]{1,0:T(8,128)}, f32[3,128,256]{2,1,0:T(8,128)}, bf16[128,1280]{1,0:T(8,128)(2,1)}, f32[3,128,256]{2,1,0:T(8,128)}, f32[128,1024]...) custom-call(bf16[128,1024]{1,0:T(8,128)(2,1)} %refs_6_.1, ...), custom_call_target="tpu_custom_call" | custom-call | tf_op jit(solution)/shard_map/node_forward/pallas_call | solution.py:801
  73.9 11.2 %exchange.5.x_ref.refs_0_ = bf16[8,192,128]{2,1,0:T(8,128)(2,1)} custom-call(bf16[8,192,128]{2,1,0:T(8,128)(2,1)} %get-tuple-element.61.x_ref), custom_call_target="tpu_custom_call" | custom-call | tf_op jit(solution)/shard_map/exchange/pallas_call | solution.py:838
  85.1 5.2 %attend.1 = (bf16[1024,1024]{1,0:T(8,128)(2,1)}, f32[1024,128]{1,0:T(8,128)}, bf16[8,64,128]{2,1,0:T(8,128)(2,1)}) custom-call(bf16[8,192,128]{2,1,0:T(8,128)(2,1)} %exchange.5.x_ref.refs_0_, s32[1,1024]{1,0:T(1,128)} %bitcast.363), custom_call_target="tpu_custom_call" | custom-call | tf_op jit(solution)/shard_map/attend/pallas_call | solution.py:891
  90.3 8.7 %exchange.6.att_ref = bf16[8,64,128]{2,1,0:T(8,128)(2,1)} custom-call(bf16[8,64,128]{2,1,0:T(8,128)(2,1)} %get-tuple-element.62.x_ref), custom_call_target="tpu_custom_call" | custom-call | tf_op jit(solution)/shard_map/exchange/pallas_call | solution.py:838
  99.0 8.7 %feed.1 = (bf16[128,512]{1,0:T(8,128)(2,1)}, bf16[8,512,512]{2,1,0:T(8,128)(2,1)}, bf16[8,64,128]{2,1,0:T(8,128)(2,1)}, f32[128,512]{1,0:T(8,128)}, bf16[128,512...) custom-call(bf16[8,64,128]{2,1,0:T(8,128)(2,1)} %exchange.6.att_ref, ...), custom_call_target="tpu_custom_call" | custom-call | tf_op jit(solution)/shard_map/feed/pallas_call | solution.py:1008
  107.7 3.0 dynamic-slice_bitcast_fusion.2
  110.9 4.2 %collective-permute-done = bf16[4,512,512]{2,1,0:T(8,128)(2,1)S(1)} collective-permute-done((bf16[4,512,512]{2,1,0:T(8,128)(2,1)}, bf16[4,512,512]{2,1,0:T(8,128)(2,1)S(1)}, u32[]{:S(2)}, u32[]{:S(2)}) %collective-permute-start) | collective-permute-done | bytes 2097184 | tf_op jit(solution)/shard_map/ppermute | solution.py:633
  115.1 2.2 fusion.2.refs_4_
  123.3 7.1 %exchange.7.refs_3_ = bf16[8,64,128]{2,1,0:T(8,128)(2,1)} custom-call(bf16[8,64,128]{2,1,0:T(8,128)(2,1)} %get-tuple-element.69.x_ref), custom_call_target="tpu_custom_call" | custom-call | tf_op jit(solution)/shard_map/exchange/pallas_call | solution.py:838
  130.4 4.8 %attend_backward.1.x_ref = bf16[8,192,128]{2,1,0:T(8,128)(2,1)} custom-call(bf16[8,192,128]{2,1,0:T(8,128)(2,1)} %exchange.5.x_ref.refs_0_, bf16[1024,1024]{1,0:T(8,128)(2,1)} %get-tuple-element.67.refs_1_, f32[1024,128]{1,0:T(8,128)} %get-tuple-element.68.refs_2_, bf16[8,64,128]{2,1,0:T(8,128)(2,1)} %exchange.7.refs_3_, bf16[4,512,512]{2,1,0:T(8,128)(2,1)} %copy-done), custom_call_target="tpu_custom_call" | custom-call | tf_op jit(solution)/shard_map/attend_backward/pallas_call | solution.py:932
  135.2 10.9 %exchange.8.refs_0_ = bf16[8,192,128]{2,1,0:T(8,128)(2,1)} custom-call(bf16[8,192,128]{2,1,0:T(8,128)(2,1)} %attend_backward.1.x_ref), custom_call_target="tpu_custom_call" | custom-call | tf_op jit(solution)/shard_map/exchange/pallas_call | solution.py:838
  150.0 11.0 %node_backward.1 = (bf16[8,768,512]{2,1,0:T(8,128)(2,1)}, f32[128,1024]{1,0:T(8,128)}, f32[3,128,256]{2,1,0:T(8,128)}, f32[8,1024]{1,0:T(8,128)}) custom-call(bf16[8,192,128]{2,1,0:T(8,128)(2,1)} %exchange.8.refs_0_, f32[128,512]{1,0:T(8,128)} %get-tuple-element.71.refs_1_, bf16[128,512]{1,0:T(8,128)(2,1)} %get-tuple-element.72.refs_2_, ...), custom_call_target="tpu_custom_call" | custom-call | tf_op jit(solution)/shard_map/node_backward/pallas_call | solution.py:1119
  161.1 3.9 dynamic-slice_bitcast_fusion
  168.3 5.6 %collective-permute-done.4 = bf16[4,64,512]{2,1,0:T(8,128)(2,1)S(1)} collective-permute-done((bf16[4,64,512]{2,1,0:T(8,128)(2,1)S(1)}, bf16[4,64,512]{2,1,0:T(8,128)(2,1)S(1)}, u32[]{:S(2)}, u32[]{:S(2)}) %collective-permute-start.4) | collective-permute-done | bytes 262176 | tf_op jit(solution)/shard_map/ppermute | solution.py:633
  175.8 5.5 %fusion.refs_8_ = bf16[4,768,512]{2,1,0:T(8,128)(2,1)} fusion(bf16[4,768,512]{2,1,0:T(8,128)(2,1)} %collective-permute-done.3, bf16[4,2,768,512]{3,2,1,0:T(8,128)(2,1)} %bitcast.289, s32[]{:T(128)S(6)} %select_n.175), kind=kLoop, calls=%fused_computation.1 | loop fusion | flops 6291456 | bytes 9437188 | tf_op jit(solution)/shard_map/convert_element_type | solution.py:640
  181.3 27.4 %scalar_backward.1 = (bf16[30,128,640]{2,1,0:T(8,128)(2,1)}, bf16[8,640,512]{2,1,0:T(8,128)(2,1)}, bf16[8,64,128]{2,1,0:T(8,128)(2,1)}, f32[128,1024]{1,0:T(8,128)}, bf16[128,1024]{1,0:T(8,128)(2,1)}) custom-call(s32[6,1,640]{2,1,0:T(1,128)} %reshape.268.refs_0_, bf16[30,128,640]{2,1,0:T(8,128)(2,1)} %get-tuple-element.65.refs_1_, ...), custom_call_target="tpu_custom_call" | custom-call | flops 12079595520 | bytes 31457280 | tf_op jit(solution)/shard_map/scalar_backward/pallas_call | solution.py:419
  208.7 3.7 dynamic-slice_bitcast_fusion.1
  222.5 11.3 %collective-permute-done.7 = bf16[4,192,512]{2,1,0:T(8,128)(2,1)} collective-permute-done((bf16[4,192,512]{2,1,0:T(8,128)(2,1)}, bf16[4,192,512]{2,1,0:T(8,128)(2,1)}, u32[]{:S(2)}, u32[]{:S(2)}) %collective-permute-start.7) | collective-permute-done | bytes 786464 | tf_op jit(solution)/shard_map/ppermute | solution.py:633
  240.3 4.9 %fusion.1.refs_14_ = bf16[4,640,512]{2,1,0:T(8,128)(2,1)} fusion(bf16[4,640,512]{2,1,0:T(8,128)(2,1)} %collective-permute-done.6, bf16[4,2,640,512]{3,2,1,0:T(8,128)(2,1)} %bitcast.291, s32[]{:T(128)S(6)} %select_n.175), kind=kLoop, calls=%fused_computation.3 | loop fusion | flops 5242880 | bytes 7864324 | tf_op jit(solution)/shard_map/convert_element_type | solution.py:640
  245.2 29.8 %vector_backward.1 = (bf16[8,128,512]{2,1,0:T(8,128)(2,1)}, f32[3,128,256]{2,1,0:T(8,128)}, bf16[128,768]{1,0:T(8,128)(2,1)}) custom-call(s32[6,1,640]{2,1,0:T(1,128)} %reshape.268.refs_0_, f32[30,128,3]{2,1,0:T(8,128)} %bitcast.287, bf16[6,3,640]{2,1,0:T(4,128)(2,1)} %copy.131.refs_2_, bf16[30,3,128,640]{3,2,1,0:T(8,128)(2,1)} %get-tuple-element.88.refs_3_, ...), custom_call_target="tpu_custom_call" | custom-call | flops 11324620800 | bytes 31457280 | tf_op jit(solution)/shard_map/vector_backward/pallas_call | solution.py:574
  283.2 15.0 %collective-permute-done.13 = bf16[4,32,512]{2,1,0:T(8,128)(2,1)S(1)} collective-permute-done((bf16[4,32,512]{2,1,0:T(8,128)(2,1)S(1)}, bf16[4,32,512]{2,1,0:T(8,128)(2,1)S(1)}, u32[]{:S(2)}, u32[]{:S(2)}) %collective-permute-start.13) | collective-permute-done | bytes 131104 | tf_op jit(solution)/shard_map/ppermute | solution.py:633
  302.0 7.4 %collective-permute-done.14 = bf16[4,96,512]{2,1,0:T(8,128)(2,1)S(1)} collective-permute-done((bf16[4,96,512]{2,1,0:T(8,128)(2,1)S(1)}, bf16[4,96,512]{2,1,0:T(8,128)(2,1)S(1)}, u32[]{:S(2)}, u32[]{:S(2)}) %collective-permute-start.14) | collective-permute-done | bytes 393248 | tf_op jit(solution)/shard_map/ppermute | solution.py:633
  312.9 2.7 collective-permute-start.18
  316.4 27.9 %exchange.9 = bf16[8,16,1792]{2,1,0:T(8,128)(2,1)} custom-call(bf16[8,16,1792]{2,1,0:T(8,128)(2,1)} %bitcast.337), custom_call_target="tpu_custom_call" | custom-call | tf_op jit(solution)/shard_map/exchange/pallas_call | solution.py:838
  346.6 2.8 collective-permute-start.19
  350.3 23.2 %collective-permute-done.19 = bf16[512,512]{1,0:T(8,128)(2,1)} collective-permute-done((bf16[512,512]{1,0:T(8,128)(2,1)}, bf16[512,512]{1,0:T(8,128)(2,1)}, u32[]{:S(2)}, u32[]{:S(2)}) %collective-permute-start.19) | collective-permute-done | bytes 524320 | tf_op jit(solution)/shard_map/ppermute | solution.py:633
  377.4 5.5 %collective-permute-done.22 = bf16[256,512]{1,0:T(8,128)(2,1)S(1)} collective-permute-done((bf16[256,512]{1,0:T(8,128)(2,1)S(1)}, bf16[256,512]{1,0:T(8,128)(2,1)S(1)}, u32[]{:S(2)}, u32[]{:S(2)}) %collective-permute-start.22) | collective-permute-done | bytes 262176 | tf_op jit(solution)/shard_map/ppermute | solution.py:633
  386.0 9.8 %collective-permute-done.23 = bf16[2,256,512]{2,1,0:T(8,128)(2,1)S(1)} collective-permute-done((bf16[2,256,512]{2,1,0:T(8,128)(2,1)S(1)}, bf16[2,256,512]{2,1,0:T(8,128)(2,1)S(1)}, u32[]{:S(2)}, u32[]{:S(2)}) %collective-permute-start.23) | collective-permute-done | bytes 524320 | tf_op jit(solution)/shard_map/ppermute | solution.py:633
  (255 shorter events, 93.5 us)
Async XLA Ops:
  1.5 11.3 %copy-start.34 = (bf16[3,3840]{1,0:T(4,128)(2,1)S(1)}, bf16[3,3840]{1,0:T(4,128)(2,1)}, u32[]{:S(2)}) copy-start(bf16[3,3840]{1,0:T(4,128)(2,1)} %param.28) | copy-start | bytes 69124
  4.6 22.5 %all-to-all-start = ((bf16[8,16,1792]{2,1,0:T(8,128)(2,1)}), bf16[8,16,1792]{2,1,0:T(8,128)(2,1)S(1)}, u32[]{:S(2)}, u32[]{:S(2)}) async-start(bf16[8,16,1792]{2,1,0:T(8,128)(2,1)} %bitcast.8), calls=%async_computation | async-start | bytes 917504 | tf_op jit(solution)/shard_map/all_to_all | solution.py:1171
  13.7 17.4 %copy-start.14 = (bf16[256,640]{1,0:T(8,128)(2,1)}, bf16[256,640]{1,0:T(8,128)(2,1)S(1)}, u32[]{:S(2)}) copy-start(bf16[256,640]{1,0:T(8,128)(2,1)S(1)} %copy.148) | copy-start | bytes 983044
  110.8 4.4 %collective-permute-start = (bf16[4,512,512]{2,1,0:T(8,128)(2,1)}, bf16[4,512,512]{2,1,0:T(8,128)(2,1)S(1)}, u32[]{:S(2)}, u32[]{:S(2)}) collective-permute-start(bf16[4,512,512]{2,1,0:T(8,128)(2,1)} %dynamic-slice_bitcast_fusion.2), channel_id=1, source_target_pairs={{0,1},{1,0},{2,3},{3,2},{4,5},{5,4},{6,7},{7,6},{8,9},{9,8},{10,11... | collective-permute-start | bytes 6291464 | tf_op jit(solution)/shard_map/ppermute | solution.py:633
  119.5 26.6 %collective-permute-start.1 = (bf16[4,128,512]{2,1,0:T(8,128)(2,1)}, bf16[4,128,512]{2,1,0:T(8,128)(2,1)}, u32[]{:S(2)}, u32[]{:S(2)}) collective-permute-start(bf16[4,128,512]{2,1,0:T(8,128)(2,1)} %dynamic-slice_bitcast_fusion.11), channel_id=1, source_target_pairs={{0,8},{8,0},{16,24},{24,16},{1,9},{9,1},{17,25},{25,17},{2,10},{10... | collective-permute-start | bytes 1572872 | tf_op jit(solution)/shard_map/ppermute | solution.py:633
  121.8 26.2 %collective-permute-start.2 = (bf16[4,128,512]{2,1,0:T(8,128)(2,1)}, bf16[4,128,512]{2,1,0:T(8,128)(2,1)}, u32[]{:S(2)}, u32[]{:S(2)}) collective-permute-start(bf16[4,128,512]{2,1,0:T(8,128)(2,1)} %dynamic-slice_bitcast_fusion.10), channel_id=1, source_target_pairs={{0,16},{8,24},{16,0},{24,8},{1,17},{9,25},{17,1},{25,9},{2,18},{10... | collective-permute-start | bytes 1572872 | tf_op jit(solution)/shard_map/ppermute | solution.py:633
  165.0 10.8 %collective-permute-start.3 = (bf16[4,768,512]{2,1,0:T(8,128)(2,1)}, bf16[4,768,512]{2,1,0:T(8,128)(2,1)}, u32[]{:S(2)}, u32[]{:S(2)}) collective-permute-start(bf16[4,768,512]{2,1,0:T(8,128)(2,1)} %dynamic-slice_bitcast_fusion), channel_id=1, source_target_pairs={{0,1},{1,0},{2,3},{3,2},{4,5},{5,4},{6,7},{7,6},{8,9},{9,8},{10,11... | collective-permute-start | bytes 9437192 | tf_op jit(solution)/shard_map/ppermute | solution.py:633
  165.6 8.3 %collective-permute-start.4 = (bf16[4,64,512]{2,1,0:T(8,128)(2,1)S(1)}, bf16[4,64,512]{2,1,0:T(8,128)(2,1)S(1)}, u32[]{:S(2)}, u32[]{:S(2)}) collective-permute-start(bf16[4,64,512]{2,1,0:T(8,128)(2,1)S(1)} %dynamic-slice_bitcast_fusion.17), channel_id=1, source_target_pairs={{0,16},{8,24},{16,0},{24,8},{1,17},{9,25},{17,1},{25,9},{2,18},{10... | collective-permute-start | bytes 786440 | tf_op jit(solution)/shard_map/ppermute | solution.py:633
  166.9 8.0 %collective-permute-start.5 = (bf16[4,64,512]{2,1,0:T(8,128)(2,1)S(1)}, bf16[4,64,512]{2,1,0:T(8,128)(2,1)S(1)}, u32[]{:S(2)}, u32[]{:S(2)}) collective-permute-start(bf16[4,64,512]{2,1,0:T(8,128)(2,1)S(1)} %dynamic-slice_bitcast_fusion.16), channel_id=1, source_target_pairs={{0,8},{8,0},{16,24},{24,16},{1,9},{9,1},{17,25},{25,17},{2,10},{10... | collective-permute-start | bytes 786440 | tf_op jit(solution)/shard_map/ppermute | solution.py:633
  212.4 27.9 %collective-permute-start.6 = (bf16[4,640,512]{2,1,0:T(8,128)(2,1)}, bf16[4,640,512]{2,1,0:T(8,128)(2,1)}, u32[]{:S(2)}, u32[]{:S(2)}) collective-permute-start(bf16[4,640,512]{2,1,0:T(8,128)(2,1)} %dynamic-slice_bitcast_fusion.1), channel_id=1, source_target_pairs={{0,1},{1,0},{2,3},{3,2},{4,5},{5,4},{6,7},{7,6},{8,9},{9,8},{10,11... | collective-permute-start | bytes 7864328 | tf_op jit(solution)/shard_map/ppermute | solution.py:633
  213.5 20.3 %collective-permute-start.7 = (bf16[4,192,512]{2,1,0:T(8,128)(2,1)}, bf16[4,192,512]{2,1,0:T(8,128)(2,1)}, u32[]{:S(2)}, u32[]{:S(2)}) collective-permute-start(bf16[4,192,512]{2,1,0:T(8,128)(2,1)} %dynamic-slice_bitcast_fusion.5), channel_id=1, source_target_pairs={{0,8},{8,0},{16,24},{24,16},{1,9},{9,1},{17,25},{25,17},{2,10},{10... | collective-permute-start | bytes 2359304 | tf_op jit(solution)/shard_map/ppermute | solution.py:633
  215.0 22.5 %collective-permute-start.8 = (bf16[4,192,512]{2,1,0:T(8,128)(2,1)}, bf16[4,192,512]{2,1,0:T(8,128)(2,1)}, u32[]{:S(2)}, u32[]{:S(2)}) collective-permute-start(bf16[4,192,512]{2,1,0:T(8,128)(2,1)} %dynamic-slice_bitcast_fusion.4), channel_id=1, source_target_pairs={{0,16},{8,24},{16,0},{24,8},{1,17},{9,25},{17,1},{25,9},{2,18},{10... | collective-permute-start | bytes 2359304 | tf_op jit(solution)/shard_map/ppermute | solution.py:633
  236.0 40.1 %collective-permute-start.9 = (bf16[4,96,512]{2,1,0:T(8,128)(2,1)}, bf16[4,96,512]{2,1,0:T(8,128)(2,1)}, u32[]{:S(2)}, u32[]{:S(2)}) collective-permute-start(bf16[4,96,512]{2,1,0:T(8,128)(2,1)} %dynamic-slice_bitcast_fusion.15), channel_id=1, source_target_pairs={{0,16},{8,24},{16,0},{24,8},{1,17},{9,25},{17,1},{25,9},{2,18},{10... | collective-permute-start | bytes 1179656 | tf_op jit(solution)/shard_map/ppermute | solution.py:633
  239.7 62.1 %collective-permute-start.10 = (bf16[4,96,512]{2,1,0:T(8,128)(2,1)}, bf16[4,96,512]{2,1,0:T(8,128)(2,1)S(1)}, u32[]{:S(2)}, u32[]{:S(2)}) collective-permute-start(bf16[4,96,512]{2,1,0:T(8,128)(2,1)} %dynamic-slice_bitcast_fusion.14), channel_id=1, source_target_pairs={{0,8},{8,0},{16,24},{24,16},{1,9},{9,1},{17,25},{25,17},{2,10},{10... | collective-permute-start | bytes 1179656 | tf_op jit(solution)/shard_map/ppermute | solution.py:633
  245.2 31.0 %copy-start.9 = (bf16[4,192,512]{2,1,0:T(8,128)(2,1)S(1)}, bf16[4,192,512]{2,1,0:T(8,128)(2,1)}, u32[]{:S(2)}) copy-start(bf16[4,192,512]{2,1,0:T(8,128)(2,1)} %copy-done.8) | copy-start | bytes 2359300
  245.2 32.8 %copy-start.2 = (bf16[4,640,512]{2,1,0:T(8,128)(2,1)S(1)}, bf16[4,640,512]{2,1,0:T(8,128)(2,1)}, u32[]{:S(2)}) copy-start(bf16[4,640,512]{2,1,0:T(8,128)(2,1)} %fusion.1.refs_14_) | copy-start | bytes 7864324
  276.1 3.7 collective-permute-start.12
  278.2 20.0 %collective-permute-start.11 = (bf16[4,160,512]{2,1,0:T(8,128)(2,1)S(1)}, bf16[4,160,512]{2,1,0:T(8,128)(2,1)S(1)}, u32[]{:S(2)}, u32[]{:S(2)}) collective-permute-start(bf16[4,160,512]{2,1,0:T(8,128)(2,1)S(1)} %dynamic-slice_bitcast_fusion.7), channel_id=1, source_target_pairs={{0,8},{8,0},{16,24},{24,16},{1,9},{9,1},{17,25},{25,17},{2,10},{10... | collective-permute-start | bytes 1966088 | tf_op jit(solution)/shard_map/ppermute | solution.py:633
  280.0 18.2 %collective-permute-start.13 = (bf16[4,32,512]{2,1,0:T(8,128)(2,1)S(1)}, bf16[4,32,512]{2,1,0:T(8,128)(2,1)S(1)}, u32[]{:S(2)}, u32[]{:S(2)}) collective-permute-start(bf16[4,32,512]{2,1,0:T(8,128)(2,1)S(1)} %dynamic-slice_bitcast_fusion.19), channel_id=1, source_target_pairs={{0,8},{8,0},{16,24},{24,16},{1,9},{9,1},{17,25},{25,17},{2,10},{10... | collective-permute-start | bytes 393224 | tf_op jit(solution)/shard_map/ppermute | solution.py:633
  281.1 18.1 %collective-permute-start.15 = (bf16[4,160,512]{2,1,0:T(8,128)(2,1)S(1)}, bf16[4,160,512]{2,1,0:T(8,128)(2,1)S(1)}, u32[]{:S(2)}, u32[]{:S(2)}) collective-permute-start(bf16[4,160,512]{2,1,0:T(8,128)(2,1)S(1)} %dynamic-slice_bitcast_fusion.6), channel_id=1, source_target_pairs={{0,16},{8,24},{16,0},{24,8},{1,17},{9,25},{17,1},{25,9},{2,18},{10... | collective-permute-start | bytes 1966088 | tf_op jit(solution)/shard_map/ppermute | solution.py:633
  281.7 19.1 %collective-permute-start.16 = (bf16[4,32,512]{2,1,0:T(8,128)(2,1)S(1)}, bf16[4,32,512]{2,1,0:T(8,128)(2,1)S(1)}, u32[]{:S(2)}, u32[]{:S(2)}) collective-permute-start(bf16[4,32,512]{2,1,0:T(8,128)(2,1)S(1)} %dynamic-slice_bitcast_fusion.18), channel_id=1, source_target_pairs={{0,16},{8,24},{16,0},{24,8},{1,17},{9,25},{17,1},{25,9},{2,18},{10... | collective-permute-start | bytes 393224 | tf_op jit(solution)/shard_map/ppermute | solution.py:633
  298.6 10.8 %collective-permute-start.14 = (bf16[4,96,512]{2,1,0:T(8,128)(2,1)S(1)}, bf16[4,96,512]{2,1,0:T(8,128)(2,1)S(1)}, u32[]{:S(2)}, u32[]{:S(2)}) collective-permute-start(bf16[4,96,512]{2,1,0:T(8,128)(2,1)S(1)} %dynamic-slice_bitcast_fusion.13), channel_id=1, source_target_pairs={{0,16},{8,24},{16,0},{24,8},{1,17},{9,25},{17,1},{25,9},{2,18},{10... | collective-permute-start | bytes 1179656 | tf_op jit(solution)/shard_map/ppermute | solution.py:633
  300.9 10.5 %collective-permute-start.17 = (bf16[4,96,512]{2,1,0:T(8,128)(2,1)S(1)}, bf16[4,96,512]{2,1,0:T(8,128)(2,1)S(1)}, u32[]{:S(2)}, u32[]{:S(2)}) collective-permute-start(bf16[4,96,512]{2,1,0:T(8,128)(2,1)S(1)} %dynamic-slice_bitcast_fusion.12), channel_id=1, source_target_pairs={{0,8},{8,0},{16,24},{24,16},{1,9},{9,1},{17,25},{25,17},{2,10},{10... | collective-permute-start | bytes 1179656 | tf_op jit(solution)/shard_map/ppermute | solution.py:633
  301.9 13.6 %copy-start.26 = (bf16[128,1024]{1,0:T(8,128)(2,1)S(1)}, bf16[128,1024]{1,0:T(8,128)(2,1)}, u32[]{:S(2)}) copy-start(bf16[128,1024]{1,0:T(8,128)(2,1)} %get-tuple-element.87) | copy-start | bytes 786436
  301.9 13.6 %copy-start.31 = (bf16[128,768]{1,0:T(8,128)(2,1)S(1)}, bf16[128,768]{1,0:T(8,128)(2,1)}, u32[]{:S(2)}) copy-start(bf16[128,768]{1,0:T(8,128)(2,1)} %get-tuple-element.95) | copy-start | bytes 589828
  312.9 31.4 %collective-permute-start.18 = (bf16[2,512,512]{2,1,0:T(8,128)(2,1)S(1)}, bf16[2,512,512]{2,1,0:T(8,128)(2,1)S(1)}, u32[]{:S(2)}, u32[]{:S(2)}) collective-permute-start(bf16[2,512,512]{2,1,0:T(8,128)(2,1)S(1)} %dynamic-slice_bitcast_fusion.3), channel_id=1, source_target_pairs={{0,2},{1,3},{2,0},{3,1},{4,6},{5,7},{6,4},{7,5},{8,10},{9,11},{10,... | collective-permute-start | bytes 3145736 | tf_op jit(solution)/shard_map/ppermute | solution.py:633
  346.6 26.9 %collective-permute-start.19 = (bf16[512,512]{1,0:T(8,128)(2,1)}, bf16[512,512]{1,0:T(8,128)(2,1)}, u32[]{:S(2)}, u32[]{:S(2)}) collective-permute-start(bf16[512,512]{1,0:T(8,128)(2,1)} %dynamic-slice_bitcast_fusion.8), channel_id=1, source_target_pairs={{0,4},{1,5},{2,6},{3,7},{4,0},{5,1},{6,2},{7,3},{8,12},{9,13},{10,... | collective-permute-start | bytes 1572872 | tf_op jit(solution)/shard_map/ppermute | solution.py:633
  350.1 24.9 %copy-start.20 = (f32[128,1024]{1,0:T(8,128)S(1)}, f32[128,1024]{1,0:T(8,128)}, u32[]{:S(2)}) copy-start(f32[128,1024]{1,0:T(8,128)} %get-tuple-element.86) | copy-start | bytes 1572868
  374.8 8.1 %collective-permute-start.22 = (bf16[256,512]{1,0:T(8,128)(2,1)S(1)}, bf16[256,512]{1,0:T(8,128)(2,1)S(1)}, u32[]{:S(2)}, u32[]{:S(2)}) collective-permute-start(bf16[256,512]{1,0:T(8,128)(2,1)S(1)} %pad_maximum_fusion.12), channel_id=1, source_target_pairs={{0,8},{8,0},{16,24},{24,16},{1,9},{9,1},{17,25},{25,17},{2,10},{10... | collective-permute-start | bytes 786440 | tf_op jit(solution)/shard_map/ppermute | solution.py:633
  375.8 8.4 %collective-permute-start.20 = (bf16[256,512]{1,0:T(8,128)(2,1)S(1)}, bf16[256,512]{1,0:T(8,128)(2,1)S(1)}, u32[]{:S(2)}, u32[]{:S(2)}) collective-permute-start(bf16[256,512]{1,0:T(8,128)(2,1)S(1)} %pad_maximum_fusion.11), channel_id=1, source_target_pairs={{0,16},{8,24},{16,0},{24,8},{1,17},{9,25},{17,1},{25,9},{2,18},{10... | collective-permute-start | bytes 786440 | tf_op jit(solution)/shard_map/ppermute | solution.py:633
  383.0 12.8 %collective-permute-start.23 = (bf16[2,256,512]{2,1,0:T(8,128)(2,1)S(1)}, bf16[2,256,512]{2,1,0:T(8,128)(2,1)S(1)}, u32[]{:S(2)}, u32[]{:S(2)}) collective-permute-start(bf16[2,256,512]{2,1,0:T(8,128)(2,1)S(1)} %pad_maximum_fusion.7), channel_id=1, source_target_pairs={{0,16},{8,24},{16,0},{24,8},{1,17},{9,25},{17,1},{25,9},{2,18},{10... | collective-permute-start | bytes 1572872 | tf_op jit(solution)/shard_map/ppermute | solution.py:633
  384.4 12.5 %collective-permute-start.21 = (bf16[2,256,512]{2,1,0:T(8,128)(2,1)S(1)}, bf16[2,256,512]{2,1,0:T(8,128)(2,1)S(1)}, u32[]{:S(2)}, u32[]{:S(2)}) collective-permute-start(bf16[2,256,512]{2,1,0:T(8,128)(2,1)S(1)} %pad_maximum_fusion.6), channel_id=1, source_target_pairs={{0,8},{8,0},{16,24},{24,16},{1,9},{9,1},{17,25},{25,17},{2,10},{10... | collective-permute-start | bytes 1572872 | tf_op jit(solution)/shard_map/ppermute | solution.py:633
  (35 other events, 171.0 us)
